TPU v7x, 512 devices: a whole 4x8x8 slice. The times are simulated.
512 devices in a mesh: slab: 16 (over x, y_hi), mode: 32 (over z, y_lo, core).
Axes of the slice: x: 4, y: 8 (y_hi: 4, y_lo: 2; y = y_hi * 2 + y_lo), z: 8, core: 2. Of those that a mesh axis runs over, the one named last changes fastest.
Arguments:
- log_coeffs: bfloat16 [192, 16, 128, 128], P('mode', 'slab'), may hold values from -0.23925781 to 0.23925781
- pressure: bfloat16 [192, 16, 128, 128], P('mode', 'slab'), may hold values from -0.41992188 to 0.41992188
- source: bfloat16 [192, 16, 128, 128], P('mode', 'slab'), may hold values from -6 to 6
- vandermonde: float32 [512, 192], replicated, may hold values from -4 to 4
- weights: float32 [512], replicated, may hold values from 0.02 to 0.2
Outputs:
- residual: bfloat16 [192, 16, 128, 128], P('mode', 'slab')
All inputs are finite; a program needn't handle non-finite values.
Results may differ from a plain program's by a relative error of at most 0.005.
Values may be sent and summed in bfloat16 or wider, within the bound.
No kernel may reach another device: no remote copies, remote signals or barrier semaphores. Data moves between devices by JAX's collectives and lax.ppermute only.
A program may use at most 64 MiB of HBM per device.

v0:
```python
import jax
import jax.numpy as jnp
from jax import lax
from jax.sharding import PartitionSpec as P


def shifted(block, axis, distance):
    devices = range(lax.axis_size(axis))
    route = [((i - distance) % len(devices), i) for i in devices]
    return lax.ppermute(block, axis, route)


def apply_matrix(matrix, field):
    flat = field.reshape(field.shape[0], -1)
    result = jnp.dot(
        matrix, flat, precision=lax.Precision.HIGHEST, preferred_element_type=jnp.float32
    )
    return result.reshape((matrix.shape[0],) + field.shape[1:])


def shards(log_coeffs, pressure, source, vandermonde, weights):
    projector = jnp.transpose(vandermonde * weights[:, None])
    upper = shifted(pressure, "slab", -1)
    extended = jnp.concatenate([pressure, upper], axis=1).astype(jnp.float32)
    base = extended[:, :-1]
    slope_z = extended[:, 1:] - base
    slope_y = jnp.roll(base, -1, axis=2) - base
    slope_x = jnp.roll(base, -1, axis=3) - base
    moved = (
        lax.all_to_all(
            log_coeffs.astype(jnp.float32), "mode", split_axis=2, concat_axis=0, tiled=True
        ),
        lax.all_to_all(slope_x, "mode", split_axis=2, concat_axis=0, tiled=True),
        lax.all_to_all(slope_y, "mode", split_axis=2, concat_axis=0, tiled=True),
        lax.all_to_all(slope_z, "mode", split_axis=2, concat_axis=0, tiled=True),
    )
    log_perm = apply_matrix(vandermonde, moved[0])
    grad_x = apply_matrix(vandermonde, moved[1])
    grad_y = apply_matrix(vandermonde, moved[2])
    grad_z = apply_matrix(vandermonde, moved[3])
    factor = jnp.exp(log_perm)
    flux_x = factor * grad_x
    flux_y = factor * grad_y
    flux_z = factor * grad_z
    back_x, back_y, back_z = (
        lax.all_to_all(
            apply_matrix(projector, flux_x), "mode", split_axis=0, concat_axis=2, tiled=True
        ),
        lax.all_to_all(
            apply_matrix(projector, flux_y), "mode", split_axis=0, concat_axis=2, tiled=True
        ),
        lax.all_to_all(
            apply_matrix(projector, flux_z), "mode", split_axis=0, concat_axis=2, tiled=True
        ),
    )
    lower = shifted(back_z.astype(jnp.bfloat16), "slab", 1).astype(back_z.dtype)
    spread = back_x - jnp.roll(back_x, 1, axis=3) + (back_y - jnp.roll(back_y, 1, axis=2))
    spread = spread + (back_z - jnp.concatenate([lower, back_z[:, :-1]], axis=1))
    return (-spread - source.astype(jnp.float32)).astype(jnp.bfloat16)


def solution(mesh):
    placed = (
        P("mode", "slab", None, None),
        P("mode", "slab", None, None),
        P("mode", "slab", None, None),
        P(),
        P(),
    )
    return jax.shard_map(
        shards, mesh=mesh, in_specs=placed, out_specs=P("mode", "slab", None, None), check_vma=False
    )
```

profile of v0, /device:TPU:1, one launch (start us, length us, event | category | flops | bytes accessed | tf_op | source)
XLA Modules:
  0.0 162.4 jit_solution(12501865156923603431)
XLA Ops:
  0.0 8.9 %collective-permute-start = (bf16[6,1,128,128]{3,2,1,0:T(8,128)(2,1)}, bf16[6,1,128,128]{3,2,1,0:T(8,128)(2,1)S(1)}, u32[]{:S(2)}, u32[]{:S(2)}) collective-permute-start(bf16[6,1,128,128]{3,2,1,0:T(8,128)(2,1)} %param.6), channel_id=1, source_target_pairs={{32,0},{64,32},{96,64},{128,96},{160,128},{192,160},{224,192},{256... | collective-permute-start | bytes 589832 | tf_op jit(solution)/shard_map/ppermute | solution.py:10
  8.9 1.8 %copy.110 = f32[6,1,128,128]{3,0,1,2:T(8,128)} copy(bf16[6,1,128,128]{3,2,1,0:T(8,128)(2,1)} %param.5) | data formatting | bytes 589824 | tf_op jit(solution)/shard_map/convert_element_type | solution.py:31
  10.8 11.7 %all-to-all-start = ((f32[6,1,128,128]{3,0,1,2:T(8,128)}), f32[6,1,128,128]{3,0,1,2:T(8,128)S(1)}, u32[]{:S(2)}, u32[]{:S(2)}) async-start(f32[6,1,128,128]{3,0,1,2:T(8,128)} %copy.110), calls=%async_computation | async-start | bytes 1048576 | tf_op jit(solution)/shard_map/all_to_all | solution.py:30
  23.1 1.0 maximum_subtract_fusion
  24.1 15.0 %all-to-all-done = f32[6,1,128,128]{3,0,1,2:T(8,128)S(1)} async-done(((f32[6,1,128,128]{3,0,1,2:T(8,128)}), f32[6,1,128,128]{3,0,1,2:T(8,128)S(1)}, u32[]{:S(2)}, u32[]{:S(2)}) %all-to-all-start) | async-done | bytes 393248 | tf_op jit(solution)/shard_map/all_to_all | solution.py:30
  39.1 21.3 %all_to_all.114 = f32[6,1,128,128]{3,0,1,2:T(8,128)S(1)} all-to-all(f32[6,1,128,128]{3,0,1,2:T(8,128)S(1)} %get-tuple-element.5), channel_id=1, replica_groups=mesh['slab'=16,'mode'=32] {'mode'}, dimensions={2} | all-to-all | bytes 786432 | tf_op jit(solution)/shard_map/all_to_all | solution.py:33
  60.4 21.0 %all_to_all.115 = f32[6,1,128,128]{3,0,1,2:T(8,128)S(1)} all-to-all(f32[6,1,128,128]{3,0,1,2:T(8,128)S(1)} %get-tuple-element.6), channel_id=1, replica_groups=mesh['slab'=16,'mode'=32] {'mode'}, dimensions={2} | all-to-all | bytes 786432 | tf_op jit(solution)/shard_map/all_to_all | solution.py:34
  81.4 4.9 %all-to-all-start.5 = ((f32[6,1,128,128]{3,0,1,2:T(8,128)}), f32[6,1,128,128]{3,0,1,2:T(8,128)S(1)}, u32[]{:S(2)}, u32[]{:S(2)}) async-start(f32[6,1,128,128]{3,0,1,2:T(8,128)} %get-tuple-element.7), calls=%async_computation.5 | async-start | bytes 1048576 | tf_op jit(solution)/shard_map/all_to_all | solution.py:35
  87.3 1.1 convolution_exponential_fusion
  88.6 1.1 fusion.12
  89.7 1.2 convolution_bitcast_fusion.2
  92.0 11.3 %all-to-all-done.5 = f32[6,1,128,128]{3,0,1,2:T(8,128)S(1)} async-done(((f32[6,1,128,128]{3,0,1,2:T(8,128)}), f32[6,1,128,128]{3,0,1,2:T(8,128)S(1)}, u32[]{:S(2)}, u32[]{:S(2)}) %all-to-all-start.5) | async-done | bytes 393248 | tf_op jit(solution)/shard_map/all_to_all | solution.py:35
  103.3 4.8 %all-to-all-start.2 = ((f32[192,1,4,128]{3,2,1,0:T(4,128)}), f32[192,1,4,128]{3,2,1,0:T(4,128)S(1)}, u32[]{:S(2)}, u32[]{:S(2)}) async-start(f32[192,1,4,128]{3,2,1,0:T(4,128)} %copy.117), calls=%async_computation.2 | async-start | bytes 786432 | tf_op jit(solution)/shard_map/all_to_all | solution.py:46
  108.3 1.1 fusion.6
  109.4 1.2 convolution_bitcast_fusion
  110.6 1.0 copy.125
  111.7 10.4 %all-to-all-done.2 = f32[192,1,4,128]{3,2,1,0:T(4,128)S(1)} async-done(((f32[192,1,4,128]{3,2,1,0:T(4,128)}), f32[192,1,4,128]{3,2,1,0:T(4,128)S(1)}, u32[]{:S(2)}, u32[]{:S(2)}) %all-to-all-start.2) | async-done | bytes 393248 | tf_op jit(solution)/shard_map/all_to_all | solution.py:46
  122.1 5.2 %all-to-all-start.6 = ((f32[192,1,4,128]{3,2,1,0:T(4,128)}), f32[192,1,4,128]{3,2,1,0:T(4,128)S(1)}, u32[]{:S(2)}, u32[]{:S(2)}) async-start(f32[192,1,4,128]{3,2,1,0:T(4,128)} %copy.125), calls=%async_computation.6 | async-start | bytes 786432 | tf_op jit(solution)/shard_map/all_to_all | solution.py:52
  127.4 1.1 fusion.9
  128.5 1.2 convolution_bitcast_fusion.1
  130.7 10.4 %all-to-all-done.6 = f32[192,1,4,128]{3,2,1,0:T(4,128)S(1)} async-done(((f32[192,1,4,128]{3,2,1,0:T(4,128)}), f32[192,1,4,128]{3,2,1,0:T(4,128)S(1)}, u32[]{:S(2)}, u32[]{:S(2)}) %all-to-all-start.6) | async-done | bytes 393248 | tf_op jit(solution)/shard_map/all_to_all | solution.py:52
  141.1 5.2 %all-to-all-start.4 = ((f32[192,1,4,128]{3,2,1,0:T(4,128)}), f32[192,1,4,128]{3,2,1,0:T(4,128)S(1)}, u32[]{:S(2)}, u32[]{:S(2)}) async-start(f32[192,1,4,128]{3,2,1,0:T(4,128)} %copy.121), calls=%async_computation.4 | async-start | bytes 786432 | tf_op jit(solution)/shard_map/all_to_all | solution.py:49
  146.4 1.9 %collective-permute-start.1 = (bf16[6,1,128,128]{3,2,0,1:T(8,128)(2,1)S(1)}, bf16[6,1,128,128]{3,2,0,1:T(8,128)(2,1)S(1)}, u32[]{:S(2)}, u32[]{:S(2)}) collective-permute-start(bf16[6,1,128,128]{3,2,0,1:T(8,128)(2,1)S(1)} %convert_element_type.28), channel_id=1, source_target_pairs={{480,0},{0,32},{32,64},{64,96},{96,128},{128,160},{160,192},{192,2... | collective-permute-start | bytes 589832 | tf_op jit(solution)/shard_map/ppermute | solution.py:10
  148.6 11.9 %all-to-all-done.4 = f32[192,1,4,128]{3,2,1,0:T(4,128)S(1)} async-done(((f32[192,1,4,128]{3,2,1,0:T(4,128)}), f32[192,1,4,128]{3,2,1,0:T(4,128)S(1)}, u32[]{:S(2)}, u32[]{:S(2)}) %all-to-all-start.4) | async-done | bytes 393248 | tf_op jit(solution)/shard_map/all_to_all | solution.py:49
  (33 shorter events, 6.2 us)
Async XLA Ops:
  0.0 22.4 %collective-permute-start = (bf16[6,1,128,128]{3,2,1,0:T(8,128)(2,1)}, bf16[6,1,128,128]{3,2,1,0:T(8,128)(2,1)S(1)}, u32[]{:S(2)}, u32[]{:S(2)}) collective-permute-start(bf16[6,1,128,128]{3,2,1,0:T(8,128)(2,1)} %param.6), channel_id=1, source_target_pairs={{32,0},{64,32},{96,64},{128,96},{160,128},{192,160},{224,192},{256... | collective-permute-start | bytes 589832 | tf_op jit(solution)/shard_map/ppermute | solution.py:10
  10.8 11.7 %copy-start.2 = (bf16[6,1,128,128]{3,2,1,0:T(8,128)(2,1)S(1)}, bf16[6,1,128,128]{3,2,1,0:T(8,128)(2,1)}, u32[]{:S(2)}) copy-start(bf16[6,1,128,128]{3,2,1,0:T(8,128)(2,1)} %param.6) | copy-start | bytes 589828
  10.8 28.4 %all-to-all-start = ((f32[6,1,128,128]{3,0,1,2:T(8,128)}), f32[6,1,128,128]{3,0,1,2:T(8,128)S(1)}, u32[]{:S(2)}, u32[]{:S(2)}) async-start(f32[6,1,128,128]{3,0,1,2:T(8,128)} %copy.110), calls=%async_computation | async-start | bytes 1048576 | tf_op jit(solution)/shard_map/all_to_all | solution.py:30
  81.4 21.9 %all-to-all-start.5 = ((f32[6,1,128,128]{3,0,1,2:T(8,128)}), f32[6,1,128,128]{3,0,1,2:T(8,128)S(1)}, u32[]{:S(2)}, u32[]{:S(2)}) async-start(f32[6,1,128,128]{3,0,1,2:T(8,128)} %get-tuple-element.7), calls=%async_computation.5 | async-start | bytes 1048576 | tf_op jit(solution)/shard_map/all_to_all | solution.py:35
  86.3 1.0 copy-start
  88.6 1.1 copy-start.3
  103.3 18.7 %all-to-all-start.2 = ((f32[192,1,4,128]{3,2,1,0:T(4,128)}), f32[192,1,4,128]{3,2,1,0:T(4,128)S(1)}, u32[]{:S(2)}, u32[]{:S(2)}) async-start(f32[192,1,4,128]{3,2,1,0:T(4,128)} %copy.117), calls=%async_computation.2 | async-start | bytes 786432 | tf_op jit(solution)/shard_map/all_to_all | solution.py:46
  122.1 19.1 %all-to-all-start.6 = ((f32[192,1,4,128]{3,2,1,0:T(4,128)}), f32[192,1,4,128]{3,2,1,0:T(4,128)S(1)}, u32[]{:S(2)}, u32[]{:S(2)}) async-start(f32[192,1,4,128]{3,2,1,0:T(4,128)} %copy.125), calls=%async_computation.6 | async-start | bytes 786432 | tf_op jit(solution)/shard_map/all_to_all | solution.py:52
  141.1 19.4 %all-to-all-start.4 = ((f32[192,1,4,128]{3,2,1,0:T(4,128)}), f32[192,1,4,128]{3,2,1,0:T(4,128)S(1)}, u32[]{:S(2)}, u32[]{:S(2)}) async-start(f32[192,1,4,128]{3,2,1,0:T(4,128)} %copy.121), calls=%async_computation.4 | async-start | bytes 786432 | tf_op jit(solution)/shard_map/all_to_all | solution.py:49
  146.4 14.2 %collective-permute-start.1 = (bf16[6,1,128,128]{3,2,0,1:T(8,128)(2,1)S(1)}, bf16[6,1,128,128]{3,2,0,1:T(8,128)(2,1)S(1)}, u32[]{:S(2)}, u32[]{:S(2)}) collective-permute-start(bf16[6,1,128,128]{3,2,0,1:T(8,128)(2,1)S(1)} %convert_element_type.28), channel_id=1, source_target_pairs={{480,0},{0,32},{32,64},{64,96},{96,128},{128,160},{160,192},{192,2... | collective-permute-start | bytes 589832 | tf_op jit(solution)/shard_map/ppermute | solution.py:10
  160.5 0.9 copy-start.1
where the time goes:
time: 164 us; the launch traced here: 162 us
  waiting for transfers between devices  59.1 us (36%)
  starting transfers between devices  42.5 us (26%)
  blocking collectives  42.3 us (26%)
  matrix products  8.06 us (5%)
  local copies, waits for them, and re-layouts  7.86 us (5%)
  other arithmetic  2.28 us (1%)
    all_to_all x1, blocking collectives, shards(): lax.all_to_all(slope_x, 'mode', split_axis=2, concat_axis=0, tiled=True)  21.3 us
    all_to_all x1, blocking collectives, shards(): lax.all_to_all(slope_y, 'mode', split_axis=2, concat_axis=0, tiled=True)  21 us
    all_to_all x1, waiting for transfers between devices, shards(): lax.all_to_all(log_coeffs.astype(jnp.float32), 'mode', split_axis=2, conc...  15 us
    all_to_all x1, waiting for transfers between devices, shards(): lax.all_to_all(apply_matrix(projector, flux_y), 'mode', split_axis=0, con...  11.9 us
    all_to_all x1, starting transfers between devices, shards(): lax.all_to_all(log_coeffs.astype(jnp.float32), 'mode', split_axis=2, conc...  11.7 us
    all_to_all x1, waiting for transfers between devices, shards(): lax.all_to_all(slope_z, 'mode', split_axis=2, concat_axis=0, tiled=True)  11.3 us
    ppermute x2, starting transfers between devices, shifted(): return lax.ppermute(block, axis, route)  10.8 us
    all_to_all x1, waiting for transfers between devices, shards(): lax.all_to_all(apply_matrix(projector, flux_x), 'mode', split_axis=0, con...  10.4 us
  transfers between devices with their start and end apart: 7, of which 5 were waited for; matrix products, arithmetic and copies ran while one was open for 10% of the time, Pallas kernels for 0%

commit v1 on v0

v1 whole, which is shorter than its diff:
```python
import functools

import jax
import jax.numpy as jnp
from jax import lax
from jax.experimental import pallas as pl
from jax.experimental.pallas import tpu as pltpu
from jax.sharding import PartitionSpec as P

F32 = jnp.float32
BF16 = jnp.bfloat16
OWN = 6
GROUP = 32
ROWS = 4
M = OWN * GROUP
Q = 512
X = 128
CELLS = ROWS * X
VMEM = 48 * 1024 * 1024


def slab_shift(block, distance):
    devices = range(lax.axis_size("slab"))
    route = [((i - distance) % len(devices), i) for i in devices]
    return lax.ppermute(block, "slab", route)


def exchange(block):
    return lax.all_to_all(block, "mode", split_axis=0, concat_axis=0, tiled=True)


def halves(values):
    high = values.astype(BF16)
    return high, (values - high.astype(F32)).astype(BF16)


def dot(a, b):
    return jnp.dot(a, b, preferred_element_type=F32)


def pack_kernel(log_ref, pressure_ref, out_ref, wide, block):
    for offset, ref in ((0, log_ref), (24, pressure_ref)):
        for m in range(OWN):
            wide[...] = ref[m].astype(F32).reshape(16, 8, X)
            at = offset + m * ROWS
            block[:, 0, at : at + ROWS, :] = wide[:, 0:4, :]
            block[:, 1, at : at + ROWS, :] = wide[:, 4:8, :]
            if offset:
                block[:, 0, 48 + m, :] = wide[:, 4, :]
                block[0:15, 1, 48 + m, :] = wide[1:16, 0, :]
                block[15:16, 1, 48 + m, :] = wide[0:1, 0, :]
    block[:, :, 54:56, :] = jnp.zeros((16, 2, 2, X), F32)
    out_ref[...] = block[...].astype(BF16)


def by_rows(rows, flat, out_ref):
    flat[...] = rows.reshape(M * ROWS, X)
    for j in range(ROWS):
        out_ref[:, j * X : (j + 1) * X] = flat[pl.ds(j, M, stride=ROWS), :].astype(BF16)


def own_kernel(
    got_ref, vander_ref, weights_ref,
    vh_ref, vl_ref, ph_ref, pl_ref, factor_ref, field_ref, local_ref, edge_ref,
    wide, flat, halo, logs, press, fields,
):
    vh, vl = halves(vander_ref[...])
    vh_ref[...] = vh
    vl_ref[...] = vl
    ph, plow = halves(jnp.transpose(vander_ref[...] * weights_ref[...]))
    ph_ref[...] = ph
    pl_ref[...] = plow
    wide[...] = got_ref[...].astype(F32)
    by_rows(wide[:, 0:24, :], flat, logs)
    by_rows(wide[:, 24:48, :], flat, press)
    for owner in range(GROUP):
        halo[owner * OWN : (owner + 1) * OWN, :] = wide[owner, 48 : 48 + OWN, :]
    press[:, CELLS : CELLS + X] = halo[...].astype(BF16)
    factor_ref[...] = jnp.exp(dot(vh_ref[...], logs[...]) + dot(vl_ref[...], logs[...]))
    fields[...] = dot(vh_ref[...], press[...]) + dot(vl_ref[...], press[...])
    field_ref[...] = fields[:, 0:CELLS]
    before = None
    for j in range(ROWS):
        here = fields[:, j * X : (j + 1) * X]
        factor = factor_ref[:, j * X : (j + 1) * X]
        flux_x = factor * (pltpu.roll(here, X - 1, 1) - here)
        flux_y = factor * (fields[:, (j + 1) * X : (j + 2) * X] - here)
        total = flux_x - pltpu.roll(flux_x, 1, 1) + flux_y
        if before is not None:
            total = total - before
        local_ref[:, j * X : (j + 1) * X] = total
        before = flux_y
    fh, fl = halves(before)
    edge_ref[...] = dot(ph_ref[...], fh) + dot(pl_ref[...], fh) + dot(ph_ref[...], fl)


def join_kernel(
    upper_ref, lower_ref, vh_ref, vl_ref, ph_ref, pl_ref, factor_ref, field_ref, local_ref, edge_ref,
    out_ref,
    wide, flat, logs, press, block,
):
    by_rows(upper_ref[...].astype(F32), flat, press)
    rise = dot(vh_ref[...], press[...]) + dot(vl_ref[...], press[...]) - field_ref[...]
    total = local_ref[...] + factor_ref[...] * rise
    wide[...] = lower_ref[...].astype(F32)
    by_rows(wide[:, 0:24, :], flat, logs)
    by_rows(wide[:, 24:48, :], flat, press)
    factor = jnp.exp(dot(vh_ref[...], logs[...]) + dot(vl_ref[...], logs[...]))
    rise = field_ref[...] - (dot(vh_ref[...], press[...]) + dot(vl_ref[...], press[...]))
    fh, fl = halves(total - factor * rise)
    spread = dot(ph_ref[...], fh) + dot(pl_ref[...], fh) + dot(ph_ref[...], fl)
    for j in range(ROWS):
        flat[pl.ds(j, M, stride=ROWS), :] = spread[:, j * X : (j + 1) * X]
    block[:, 0:24, :] = flat[...].reshape(GROUP, 24, X)
    for owner in range(GROUP):
        block[owner, 24 : 24 + OWN, :] = edge_ref[owner * OWN : (owner + 1) * OWN, :]
    block[:, 30:32, :] = jnp.zeros((GROUP, 2, X), F32)
    out_ref[...] = block[...].astype(BF16)


def finish_kernel(got_ref, source_ref, out_ref, wide, plane):
    wide[...] = got_ref[...].astype(F32)
    for m in range(OWN):
        at = m * ROWS
        plane[:, 0:4, :] = wide[:, 0, at : at + ROWS, :]
        plane[:, 4:8, :] = wide[:, 1, at : at + ROWS, :]
        plane[0:1, 0, :] -= wide[15:16, 1, 24 + m, :]
        plane[1:16, 0, :] -= wide[0:15, 1, 24 + m, :]
        plane[:, 4, :] -= wide[:, 0, 24 + m, :]
        out_ref[m] = (-plane[...].reshape(X, X) - source_ref[m].astype(F32)).astype(BF16)


def call(kernel, outs, scratch, cost):
    outs = [jax.ShapeDtypeStruct(shape, dtype) for shape, dtype in outs]
    return pl.pallas_call(
        kernel,
        out_shape=outs if len(outs) > 1 else outs[0],
        scratch_shapes=[pltpu.VMEM(shape, dtype) for shape, dtype in scratch],
        compiler_params=pltpu.CompilerParams(vmem_limit_bytes=VMEM),
        cost_estimate=pl.CostEstimate(flops=cost, bytes_accessed=2**20, transcendentals=0),
    )


def shards(log_coeffs, pressure, source, vandermonde, weights):
    plane = (OWN, X, X)
    packed = call(
        pack_kernel,
        [((16, 2, 56, X), BF16)],
        [((16, 8, X), F32), ((16, 2, 56, X), F32)],
        10**6,
    )(log_coeffs.reshape(plane), pressure.reshape(plane))
    got = exchange(packed.reshape(GROUP, 56, X))
    upper = slab_shift(got[:, 24:48], -1)
    lower = slab_shift(got[:, 0:48], 1)
    own = call(
        own_kernel,
        [
            ((Q, M), BF16), ((Q, M), BF16), ((M, Q), BF16), ((M, Q), BF16),
            ((Q, CELLS), F32), ((Q, CELLS), F32), ((Q, CELLS), F32), ((M, X), F32),
        ],
        [
            ((GROUP, 56, X), F32), ((M * ROWS, X), F32), ((M, X), F32),
            ((M, CELLS), BF16), ((M, CELLS + X), BF16), ((Q, CELLS + X), F32),
        ],
        10**9,
    )(got, vandermonde, weights.reshape(Q, 1))
    back = call(
        join_kernel,
        [((GROUP, 32, X), BF16)],
        [
            ((GROUP, 48, X), F32), ((M * ROWS, X), F32),
            ((M, CELLS), BF16), ((M, CELLS), BF16), ((GROUP, 32, X), F32),
        ],
        10**9,
    )(upper, lower, *own)
    returned = exchange(back)
    result = call(
        finish_kernel,
        [(plane, BF16)],
        [((16, 2, 32, X), F32), ((16, 8, X), F32)],
        10**6,
    )(returned.reshape(16, 2, 32, X), source.reshape(plane))
    return result.reshape(OWN, 1, X, X)


def solution(mesh):
    placed = (
        P("mode", "slab", None, None),
        P("mode", "slab", None, None),
        P("mode", "slab", None, None),
        P(),
        P(),
    )
    return jax.shard_map(
        shards, mesh=mesh, in_specs=placed, out_specs=P("mode", "slab", None, None), check_vma=False
    )
```

time: 164 us -> 74.4 us (0.45)
  waiting for transfers between devices: 59.1 us -> 3.23 us
  starting transfers between devices: 42.5 us -> 9.63 us
  blocking collectives: 42.3 us -> 53.8 us
  matrix products: 8.06 us -> 0 us
  local copies, waits for them, and re-layouts: 7.86 us -> 2.73 us
  Pallas kernels: 0 us -> 4.58 us
  other arithmetic: 2.28 us -> 0 us
    all_to_all x5 -> x0, waiting for transfers between devices: 59.1 us -> none  [the longest x1 15 us: shards(): lax.all_to_all(log_coeffs.astype(jnp.float32), 'mode', split_axis=2, conc...]
    all_to_all x5 -> x0, starting transfers between devices: 31.7 us -> none  [the longest x1 11.7 us: shards(): lax.all_to_all(log_coeffs.astype(jnp.float32), 'mode', split_axis=2, conc...]
    all_to_all x2, blocking collectives: 42.3 us -> 53.8 us  [exchange(): lax.all_to_all(block, 'mode', split_axis=0, concat_axis=0, tiled=True)]
    dot_general x7 -> x0, matrix products: 8.06 us -> none  [apply_matrix(): jnp.dot(matrix, flat, precision=lax.Precision.HIGHEST, preferred_element_...]
    pallas_call x0 -> x4, Pallas kernels: none -> 4.58 us  [the longest x1 1.74 us: shards(): call(join_kernel, [((GROUP, 32, X), BF16)], [((GROUP, 48, X), F32), ((M *...]
    ppermute x2, waiting for transfers between devices: 0.01 us -> 3.23 us  [slab_shift(): return lax.ppermute(block, 'slab', route)]
    dot_general x3 -> x0, local copies, waits for them, and re-layouts: 3.03 us -> none  [apply_matrix(): jnp.dot(matrix, flat, precision=lax.Precision.HIGHEST, preferred_element_...]
    convert_element_type x1 -> x0, local copies, waits for them, and re-layouts: 1.85 us -> none  [shards(): log_coeffs.astype(jnp.float32)]
  transfers between devices with their start and end apart: 7 -> 2, of which waited for: 5 -> 2; matrix products, arithmetic and copies ran while one was open for 10% -> 0% of each run, Pallas kernels for 0% -> 2%
where the time goes in v1:
time: 74.4 us; the launch traced here: 74.1 us
  blocking collectives  53.8 us (72%)
  starting transfers between devices  9.63 us (13%)
  Pallas kernels  4.58 us (6%)
  waiting for transfers between devices  3.23 us (4%)
  local copies, waits for them, and re-layouts  2.73 us (4%)
    all_to_all x2, blocking collectives, exchange(): lax.all_to_all(block, 'mode', split_axis=0, concat_axis=0, tiled=True)  53.8 us
    ppermute x2, starting transfers between devices, slab_shift(): return lax.ppermute(block, 'slab', route)  9.63 us
    ppermute x2, waiting for transfers between devices, slab_shift(): return lax.ppermute(block, 'slab', route)  3.23 us
    unnamed x11, local copies, waits for them, and re-layouts  2.53 us
    pallas_call x1, Pallas kernels, shards(): call(join_kernel, [((GROUP, 32, X), BF16)], [((GROUP, 48, X), F32), ((M *...  1.74 us
    pallas_call x1, Pallas kernels, shards(): call(own_kernel, [((Q, M), BF16), ((Q, M), BF16), ((M, Q), BF16), ((M, Q)...  1.58 us
  transfers between devices with their start and end apart: 2, of which 2 were waited for; matrix products, arithmetic and copies ran while one was open for 0% of the time, Pallas kernels for 2%

profile of v1, /device:TPU:1, one launch (start us, length us, event | category | flops | bytes accessed | tf_op | source)
XLA Modules:
  0.0 74.1 jit_solution(8847775143775973112)
XLA Ops:
  0.0 0.0 copy-start.1
  0.0 0.9 %copy-done.1 = bf16[6,1,128,128]{3,2,1,0:T(8,128)(2,1)S(1)} copy-done((bf16[6,1,128,128]{3,2,1,0:T(8,128)(2,1)S(1)}, bf16[6,1,128,128]{3,2,1,0:T(8,128)(2,1)}, u32[]{:S(2)}) %copy-start.1) | copy-done | bytes 196632
  0.9 0.0 copy-start.2
  0.9 0.9 %copy-done.2 = bf16[6,1,128,128]{3,2,1,0:T(8,128)(2,1)S(1)} copy-done((bf16[6,1,128,128]{3,2,1,0:T(8,128)(2,1)S(1)}, bf16[6,1,128,128]{3,2,1,0:T(8,128)(2,1)}, u32[]{:S(2)}) %copy-start.2) | copy-done | bytes 196632
  1.9 0.3 shard_map.55
  2.2 28.0 %all_to_all.10.got_ref = bf16[32,56,128]{2,1,0:T(8,128)(2,1)S(1)} all-to-all(bf16[32,56,128]{2,1,0:T(8,128)(2,1)S(1)} %bitcast.9), channel_id=1, replica_groups=mesh['slab'=16,'mode'=32] {'mode'}, dimensions={0} | all-to-all | bytes 917504 | tf_op jit(solution)/shard_map/all_to_all | solution.py:29
  30.2 0.0 copy-start.3
  30.2 4.3 %collective-permute-start.1 = (bf16[32,48,128]{2,1,0:T(8,128)(2,1)S(1)}, bf16[32,48,128]{2,1,0:T(8,128)(2,1)S(1)}, u32[]{:S(2)}, u32[]{:S(2)}) collective-permute-start(bf16[32,48,128]{2,1,0:T(8,128)(2,1)S(1)} %slice.9), channel_id=1, source_target_pairs={{480,0},{0,32},{32,64},{64,96},{96,128},{128,160},{160,192},{192,2... | collective-permute-start | bytes 1179656 | tf_op jit(solution)/shard_map/ppermute | solution.py:25
  34.6 5.3 %collective-permute-start = (bf16[32,24,128]{2,1,0:T(8,128)(2,1)S(1)}, bf16[32,24,128]{2,1,0:T(8,128)(2,1)S(1)}, u32[]{:S(2)}, u32[]{:S(2)}) collective-permute-start(bf16[32,24,128]{2,1,0:T(8,128)(2,1)S(1)} %slice.8), channel_id=1, source_target_pairs={{32,0},{64,32},{96,64},{128,96},{160,128},{192,160},{224,192},{256... | collective-permute-start | bytes 589832 | tf_op jit(solution)/shard_map/ppermute | solution.py:25
  39.8 0.0 copy-done.3
  39.9 0.0 copy-start.4
  39.9 0.2 copy.8.vander_ref
  40.1 0.5 copy-done.4
  40.5 0.1 copy.9.weights_ref
  40.7 1.6 %shard_map.56 = (bf16[512,192]{1,0:T(8,128)(2,1)S(1)}, bf16[512,192]{1,0:T(8,128)(2,1)S(1)}, bf16[192,512]{1,0:T(8,128)(2,1)S(1)}, bf16[192,512]{1,0:T(8,128)(2,...) custom-call(bf16[32,56,128]{2,1,0:T(8,128)(2,1)S(1)} %all_to_all.10.g, ...), custom_call_target="tpu_custom_call" | custom-call | flops 1000000000 | bytes 1048576 | tf_op jit(solution)/shard_map/pallas_call | solution.py:155
  42.3 2.9 %collective-permute-done.upper_ref = bf16[32,24,128]{2,1,0:T(8,128)(2,1)S(1)} collective-permute-done((bf16[32,24,128]{2,1,0:T(8,128)(2,1)S(1)}, bf16[32,24,128]{2,1,0:T(8,128)(2,1)S(1)}, u32[]{:S(2)}, u32[]{:S(2)}) %collective-permute-start) | collective-permute-done | bytes 196640 | tf_op jit(solution)/shard_map/ppermute | solution.py:25
  45.2 0.3 collective-permute-done.1.lower_ref
  45.5 1.7 %shard_map.57 = bf16[32,32,128]{2,1,0:T(8,128)(2,1)S(1)} custom-call(bf16[32,24,128]{2,1,0:T(8,128)(2,1)S(1)} %collective-permute-done.upper_ref, bf16[32,48,128]{2,1,0:T(8,128)(2,1)S(1)} %collective-permute-done.1.lower_ref, bf16[512,192]{1,0:T(8,128)(2,1)S(1)} %get-tuple-element.13.vh_ref, bf16[512,192]{1,0:T(8,128)(2,1)S(1)} %get-tuple-element.14.vl_ref, ...), custom_call_target="tpu_custom_call" | custom-call | flops 1000000000 | bytes 1048576 | tf_op jit(solution)/shard_map/pallas_call | solution.py:167
  47.3 0.0 copy-start
  47.3 25.8 %all_to_all.11 = bf16[32,32,128]{2,1,0:T(8,128)(2,1)S(1)} all-to-all(bf16[32,32,128]{2,1,0:T(8,128)(2,1)S(1)} %shard_map.57), channel_id=1, replica_groups=mesh['slab'=16,'mode'=32] {'mode'}, dimensions={0} | all-to-all | bytes 524288 | tf_op jit(solution)/shard_map/all_to_all | solution.py:29
  73.1 0.0 copy-done
  73.1 1.0 %shard_map.58 = bf16[6,128,128]{2,1,0:T(8,128)(2,1)} custom-call(bf16[16,2,32,128]{3,2,1,0:T(8,128)(2,1)S(1)} %bitcast.10, bf16[6,128,128]{2,1,0:T(8,128)(2,1)S(1)} %bitcast.11), custom_call_target="tpu_custom_call" | custom-call | flops 1000000 | bytes 1048576 | tf_op jit(solution)/shard_map/pallas_call | solution.py:177
  (2 shorter events, 0.0 us)
Async XLA Ops:
  0.0 0.9 %copy-start.1 = (bf16[6,1,128,128]{3,2,1,0:T(8,128)(2,1)S(1)}, bf16[6,1,128,128]{3,2,1,0:T(8,128)(2,1)}, u32[]{:S(2)}) copy-start(bf16[6,1,128,128]{3,2,1,0:T(8,128)(2,1)} %param.5) | copy-start | bytes 589828
  0.9 0.9 %copy-start.2 = (bf16[6,1,128,128]{3,2,1,0:T(8,128)(2,1)S(1)}, bf16[6,1,128,128]{3,2,1,0:T(8,128)(2,1)}, u32[]{:S(2)}) copy-start(bf16[6,1,128,128]{3,2,1,0:T(8,128)(2,1)} %param.6) | copy-start | bytes 589828
  30.2 9.7 %copy-start.3 = (f32[512,192]{0,1:T(8,128)S(1)}, f32[512,192]{0,1:T(8,128)}, u32[]{:S(2)}) copy-start(f32[512,192]{0,1:T(8,128)} %param.8) | copy-start | bytes 1179652
  30.2 15.3 %collective-permute-start.1 = (bf16[32,48,128]{2,1,0:T(8,128)(2,1)S(1)}, bf16[32,48,128]{2,1,0:T(8,128)(2,1)S(1)}, u32[]{:S(2)}, u32[]{:S(2)}) collective-permute-start(bf16[32,48,128]{2,1,0:T(8,128)(2,1)S(1)} %slice.9), channel_id=1, source_target_pairs={{480,0},{0,32},{32,64},{64,96},{96,128},{128,160},{160,192},{192,2... | collective-permute-start | bytes 1179656 | tf_op jit(solution)/shard_map/ppermute | solution.py:25
  34.6 10.6 %collective-permute-start = (bf16[32,24,128]{2,1,0:T(8,128)(2,1)S(1)}, bf16[32,24,128]{2,1,0:T(8,128)(2,1)S(1)}, u32[]{:S(2)}, u32[]{:S(2)}) collective-permute-start(bf16[32,24,128]{2,1,0:T(8,128)(2,1)S(1)} %slice.8), channel_id=1, source_target_pairs={{32,0},{64,32},{96,64},{128,96},{160,128},{192,160},{224,192},{256... | collective-permute-start | bytes 589832 | tf_op jit(solution)/shard_map/ppermute | solution.py:25
  39.9 0.7 copy-start.4
  47.3 25.8 %copy-start = (bf16[6,1,128,128]{3,2,1,0:T(8,128)(2,1)S(1)}, bf16[6,1,128,128]{3,2,1,0:T(8,128)(2,1)}, u32[]{:S(2)}) copy-start(bf16[6,1,128,128]{3,2,1,0:T(8,128)(2,1)} %param.7) | copy-start | bytes 589828

commit v2 on v0

v2 whole, which is shorter than its diff:
```python
import jax
import jax.numpy as jnp
from jax import lax
from jax.experimental import pallas as pl
from jax.experimental.pallas import tpu as pltpu
from jax.sharding import Mesh
from jax.sharding import PartitionSpec as P

F32 = jnp.float32
BF16 = jnp.bfloat16
OWN = 6
OWNERS = 32
M = OWN * OWNERS
Q = 512
X = 128
PLANES = 4
ROWS = 4
COLS = 32
ACROSS = 4
DOWN = 32
CELLS = PLANES * X
SENT = 14
VMEM = 48 * 1024 * 1024


def halves(values):
    high = values.astype(BF16)
    return high, (values - high.astype(F32)).astype(BF16)


def dot(a, b):
    return jnp.dot(a, b, preferred_element_type=F32)


def expand(vh_ref, vl_ref, field):
    return dot(vh_ref[...], field) + dot(vl_ref[...], field)


def project(ph_ref, pl_ref, flux):
    fh, fl = halves(flux)
    return dot(ph_ref[...], fh) + dot(pl_ref[...], fh) + dot(ph_ref[...], fl)


def lane_of(rows):
    return lax.broadcasted_iota(jnp.int32, (rows, X), 1)


def turn(values, lanes):
    lanes = lanes % X
    return pltpu.roll(values, lanes, 1) if lanes else values


def grid_of(rows, columns):
    return tuple(lax.broadcasted_iota(jnp.int32, (rows, columns), axis) for axis in (0, 1))


def select(flags):
    return flags.astype(F32).astype(BF16)


def swapper():
    row, col = grid_of(4 * X, 4 * X)
    return select(row == col % X // COLS * X + col // X * COLS + col % COLS)


def start_all(copies):
    for copy in copies:
        copy.start()
    return copies


def pack_kernel(log_any, pressure_any, out_ref, planes, flat, ring, swap, shift, cells, heads, block, sems):
    copies = start_all([
        pltpu.make_async_copy(ref.at[m], planes.at[field, m], sems.at[field, m])
        for field, ref in enumerate((log_any, pressure_any))
        for m in range(OWN)
    ])
    swap[...] = swapper()
    row, col = grid_of(X, X)
    for m in range(OWN):
        shift[m * X : (m + 1) * X, :] = select((col % COLS == 26 + m) & (row == col - 26 - m))
    for field in range(2):
        for m in range(OWN):
            copies[field * OWN + m].wait()
            flat[...] = planes[field, m].astype(F32)
            rows = slice((field * OWN + m) * DOWN, (field * OWN + m + 1) * DOWN)
            for j in range(ROWS):
                cells[rows, j * X : (j + 1) * X] = flat[pl.ds(j, DOWN, stride=ROWS), :].astype(BF16)
            if field:
                ring[0:DOWN, :] = flat[pl.ds(0, DOWN, stride=ROWS), :]
                ring[DOWN : DOWN + 1, :] = flat[0:1, :]
                after = ring[1 : DOWN + 1, :]
                if m < 4:
                    cells[2 * M : 2 * M + DOWN, m * X : (m + 1) * X] = after.astype(BF16)
                else:
                    at = 2 * (m - 4) * X
                    cells[2 * M + DOWN :, at : at + X] = after.astype(BF16)
                    cells[2 * M + DOWN :, at + X : at + 2 * X] = turn(after, -16).astype(BF16)
    swapped = dot(cells[...], swap[...])
    for b in range(ACROSS):
        start = SENT * DOWN * b
        for field, offset in enumerate((0, 8)):
            for m in range(OWN):
                rows = slice((field * OWN + m) * DOWN, (field * OWN + m + 1) * DOWN)
                total = swapped[rows, b * X : (b + 1) * X]
                block[pl.ds(start + offset + m, DOWN, stride=SENT), :] = total
                if field:
                    left = (b - 1) % ACROSS
                    heads[left * DOWN : (left + 1) * DOWN, m * X : (m + 1) * X] = total.astype(BF16)
        block[pl.ds(start + 6, DOWN, stride=SENT), :] = swapped[2 * M : 2 * M + DOWN, b * X : (b + 1) * X]
    rights = dot(heads[...], shift[...])
    within = lane_of(DOWN) % COLS
    for b in range(ACROSS):
        ends = swapped[2 * M + DOWN :, b * X : (b + 1) * X]
        total = jnp.where(within < 16, ends, rights[b * DOWN : (b + 1) * DOWN])
        block[pl.ds(SENT * DOWN * b + 7, DOWN, stride=SENT), :] = total
    out_ref[...] = block[...].astype(BF16)


def own_kernel(
    got_ref, vander_ref, weights_ref,
    vh_ref, vl_ref, ph_ref, pl_ref, factor_ref, field_ref, block_ref,
    wide, turned, ordered, logs, press, right, below, cells, ends, edges, columns,
):
    for c in range(Q // X):
        points = slice(c * X, (c + 1) * X)
        turned[...] = jnp.transpose(vander_ref[points, :])
        for m in range(OWN):
            ordered[m * OWNERS : (m + 1) * OWNERS, points] = turned[pl.ds(m, OWNERS, stride=OWN), :]
    vh_ref[...], vl_ref[...] = halves(jnp.transpose(ordered[...]))
    ph_ref[...], pl_ref[...] = halves(ordered[...] * weights_ref[...])
    row, col = grid_of(X, X)
    within = col % COLS
    for m in range(4):
        columns[:, m * X : (m + 1) * X] = select((col >= 96) & (row == col - 96 + COLS * m))
    for m in range(OWN):
        at = (4 + m) * X
        columns[:, at : at + X] = select((within == COLS - 1) & (row == col - 5 + m))
    for m in range(4, OWN):
        at = (6 + m) * X
        half = jnp.where(col >= 112, 80, 96)
        columns[:, at : at + X] = select((col >= 96) & (row == col - half + 64 * (m - 4)))
    wide[...] = got_ref[...].astype(F32)
    for k in range(PLANES):
        lanes = slice(k * X, (k + 1) * X)
        for r in range(2):
            ends[r, k * OWNERS : (k + 1) * OWNERS, :] = wide[
                pl.ds(SENT * OWNERS * k + 6 + r, OWNERS, stride=SENT), :
            ].astype(BF16)
        for m in range(OWN):
            modes = slice(m * OWNERS, (m + 1) * OWNERS)
            logs[modes, lanes] = wide[pl.ds(SENT * OWNERS * k + m, OWNERS, stride=SENT), :].astype(BF16)
            here = wide[pl.ds(SENT * OWNERS * k + 8 + m, OWNERS, stride=SENT), :].astype(BF16)
            press[modes, lanes] = here
            cells[k * M + m * OWNERS : k * M + (m + 1) * OWNERS, :] = here
    next_x = dot(cells[...], select((within < COLS - 1) & (row == col + 1)))
    next_y = dot(cells[...], select(row == col + COLS))
    past_y = dot(ends[0], columns[:, 0 : 4 * X])
    past = dot(ends[1], columns[:, 4 * X :])
    for k in range(PLANES):
        lanes = slice(k * X, (k + 1) * X)
        owners = slice(k * OWNERS, (k + 1) * OWNERS)
        for m in range(OWN):
            modes = slice(m * OWNERS, (m + 1) * OWNERS)
            rows = slice(k * M + m * OWNERS, k * M + (m + 1) * OWNERS)
            right[modes, lanes] = (next_x[rows] + past[owners, m * X : (m + 1) * X]).astype(BF16)
            if m < 4:
                after = past_y[owners, m * X : (m + 1) * X]
            else:
                after = past[owners, (m + 2) * X : (m + 3) * X]
            below[modes, lanes] = (next_y[rows] + after).astype(BF16)
    factor_ref[...] = jnp.exp(expand(vh_ref, vl_ref, logs[...]))
    field_ref[...] = expand(vh_ref, vl_ref, press[...])
    flux_x = factor_ref[...] * (expand(vh_ref, vl_ref, right[...]) - field_ref[...])
    proj_x = project(ph_ref, pl_ref, flux_x)
    flux_y = factor_ref[...] * (expand(vh_ref, vl_ref, below[...]) - field_ref[...])
    proj_y = project(ph_ref, pl_ref, flux_y)
    inner = CELLS - X
    flux_z = factor_ref[:, 0:inner] * (field_ref[:, X:CELLS] - field_ref[:, 0:inner])
    proj_z = project(ph_ref, pl_ref, flux_z)
    xh, xl = halves(proj_x)
    yh, yl = halves(proj_y)
    less_x = (row == col).astype(F32) - ((within > 0) & (row == col - 1)).astype(F32)
    less_x = less_x.astype(BF16)
    less_y = ((row == col).astype(F32) - (row == col - COLS).astype(F32)).astype(BF16)
    for k in range(PLANES):
        lanes = slice(k * X, (k + 1) * X)
        owners = slice(k * OWNERS, (k + 1) * OWNERS)
        total = dot(xh[:, lanes], less_x) + dot(xl[:, lanes], less_x)
        total = total + dot(yh[:, lanes], less_y) + dot(yl[:, lanes], less_y)
        if k < PLANES - 1:
            total = total + proj_z[:, lanes]
        if k > 0:
            total = total - proj_z[:, (k - 1) * X : k * X]
        for m in range(OWN):
            modes = slice(m * OWNERS, (m + 1) * OWNERS)
            block_ref[owners, m, :] = total[modes]
            at = (m if m < 4 else 6 + m) * X
            edges[owners, at : at + X] = yh[modes, lanes]
            edges[owners, (4 + m) * X : (5 + m) * X] = xh[modes, lanes]
    back = (((1,), (1,)), ((), ()))
    block_ref[:, 6, :] = lax.dot_general(
        edges[:, 0 : 4 * X], columns[:, 0 : 4 * X], back, preferred_element_type=F32
    )
    block_ref[:, 7, :] = lax.dot_general(
        edges[:, 4 * X :], columns[:, 4 * X :], back, preferred_element_type=F32
    )


def join_kernel(
    upper_ref, lower_ref, vh_ref, vl_ref, ph_ref, pl_ref, factor_ref, field_ref, block_ref,
    out_ref,
    wide, above, faces, block,
):
    above[...] = upper_ref[...].astype(F32)
    wide[...] = lower_ref[...].astype(F32)
    for m in range(OWN):
        modes = slice(m * OWNERS, (m + 1) * OWNERS)
        faces[modes, 0:X] = above[pl.ds(m, OWNERS, stride=OWN), :].astype(BF16)
        faces[modes, X : 2 * X] = wide[pl.ds(m, OWNERS, stride=SENT), :].astype(BF16)
        faces[modes, 2 * X : 3 * X] = wide[pl.ds(8 + m, OWNERS, stride=SENT), :].astype(BF16)
    last = slice(CELLS - X, CELLS)
    values = expand(vh_ref, vl_ref, faces[...])
    top = factor_ref[:, last] * (values[:, 0:X] - field_ref[:, last])
    bottom = jnp.exp(values[:, X : 2 * X]) * (field_ref[:, 0:X] - values[:, 2 * X : 3 * X])
    both = project(ph_ref, pl_ref, jnp.concatenate([bottom, top], axis=1))
    block[...] = block_ref[...]
    for m in range(OWN):
        modes = slice(m * OWNERS, (m + 1) * OWNERS)
        block[0:OWNERS, m, :] -= both[modes, 0:X]
        block[3 * OWNERS : 4 * OWNERS, m, :] += both[modes, X : 2 * X]
    out_ref[...] = block[...].astype(BF16)


def finish_kernel(got_ref, source_ref, out_any, wide, ring, swap, shift, cells, ends, flat, planes, sems):
    swap[...] = swapper()
    row, col = grid_of(X, X)
    within = col % COLS
    for m in range(OWN):
        here = select((within == 0) & (row == (col + X - COLS) % X + 26 + m))
        shift[:, m * X : (m + 1) * X] = here
    wide[...] = got_ref[...].astype(F32)
    for b in range(ACROSS):
        lanes = slice(b * X, (b + 1) * X)
        for m in range(OWN):
            cells[m * DOWN : (m + 1) * DOWN, lanes] = wide[b, :, m, :].astype(BF16)
        cells[M : M + DOWN, lanes] = wide[b, :, 7, :].astype(BF16)
        for r in range(2):
            ring[1 : DOWN + 1, :] = wide[b, :, 6 + r, :]
            ring[0:1, :] = wide[b, DOWN - 1 : DOWN, 6 + r, :]
            at = M + (1 + r) * DOWN
            cells[at : at + DOWN, lanes] = ring[0:DOWN, :].astype(BF16)
    swapped = dot(cells[...], swap[...])
    for j in range(ROWS):
        ends[j * DOWN : (j + 1) * DOWN, :] = swapped[M : M + DOWN, j * X : (j + 1) * X].astype(BF16)
    beside = dot(ends[...], shift[...])
    above = swapped[M + DOWN : M + 2 * DOWN]
    halved = swapped[M + 2 * DOWN :]
    inside = lane_of(DOWN) % COLS < 16
    copies = []
    for m in range(OWN):
        modes = slice(m * DOWN, (m + 1) * DOWN)
        for j in range(ROWS):
            total = swapped[modes, j * X : (j + 1) * X]
            total = total - beside[j * DOWN : (j + 1) * DOWN, m * X : (m + 1) * X]
            if j == 0 and m < 4:
                total = total - above[:, m * X : (m + 1) * X]
            elif j == 0:
                at = 2 * (m - 4) * X
                far = turn(halved[:, at + X : at + 2 * X], 16)
                total = total - jnp.where(inside, halved[:, at : at + X], far)
            flat[pl.ds(j, DOWN, stride=ROWS), :] = total
        planes[m] = (-flat[...] - source_ref[m].astype(F32)).astype(BF16)
        copies.append(pltpu.make_async_copy(planes.at[m], out_any.at[m], sems.at[m]))
        copies[m].start()
    for copy in copies:
        copy.wait()


def call(kernel, outs, scratch, cost, **rest):
    outs = [jax.ShapeDtypeStruct(shape, dtype) for shape, dtype in outs]
    scratch = [pltpu.VMEM(*entry) if isinstance(entry, tuple) else entry for entry in scratch]
    return pl.pallas_call(
        kernel,
        out_shape=outs if len(outs) > 1 else outs[0],
        scratch_shapes=scratch,
        compiler_params=pltpu.CompilerParams(vmem_limit_bytes=VMEM),
        cost_estimate=pl.CostEstimate(flops=cost, bytes_accessed=2**20, transcendentals=0),
        **rest,
    )


def neighbour(block, distance):
    devices = range(lax.axis_size("x"))
    route = [((i - distance) % len(devices), i) for i in devices]
    return lax.ppermute(block, "x", route)


def exchange(block):
    return lax.all_to_all(block, ("y", "mode"), split_axis=0, concat_axis=0, tiled=True)


def shards(log_coeffs, pressure, source, vandermonde, weights):
    plane = (OWN, X, X)
    group = PLANES * OWNERS
    in_hbm = pl.BlockSpec(memory_space=pltpu.HBM)
    packed = call(
        pack_kernel,
        [((group * SENT, X), BF16)],
        [
            ((2, *plane), BF16), ((X, X), F32), ((DOWN + 8, X), F32),
            ((4 * X, 4 * X), BF16), ((OWN * X, X), BF16), ((2 * M + 2 * DOWN, 4 * X), BF16),
            ((ACROSS * DOWN, OWN * X), BF16), ((group * SENT, X), F32), pltpu.SemaphoreType.DMA((2, OWN)),
        ],
        10**6,
        in_specs=[in_hbm] * 2,
    )(*[pltpu.with_memory_space_constraint(field.reshape(plane), pltpu.HBM) for field in (log_coeffs, pressure)])
    got = exchange(packed.reshape(group, SENT // 2, 2, X))
    upper = neighbour(got[0:OWNERS, 4:7], -1).reshape(M, X)
    lower = neighbour(got[group - OWNERS : group], 1).reshape(OWNERS * SENT, X)
    own = call(
        own_kernel,
        [
            ((Q, M), BF16), ((Q, M), BF16), ((M, Q), BF16), ((M, Q), BF16),
            ((Q, CELLS), F32), ((Q, CELLS), F32), ((group, 8, X), F32),
        ],
        [
            ((group * SENT, X), F32), ((M, X), F32), ((M, Q), F32),
            ((M, CELLS), BF16), ((M, CELLS), BF16), ((M, CELLS), BF16), ((M, CELLS), BF16),
            ((PLANES * M, X), BF16), ((2, group, X), BF16), ((group, 12 * X), BF16), ((X, 12 * X), BF16),
        ],
        10**9,
    )(got.reshape(group * SENT, X), vandermonde, weights.reshape(1, Q))
    back = call(
        join_kernel,
        [((group, 8, X), BF16)],
        [((OWNERS * SENT, X), F32), ((M, X), F32), ((M, 3 * X), BF16), ((group, 8, X), F32)],
        10**9,
    )(upper, lower, *own)
    returned = exchange(back)
    result = call(
        finish_kernel,
        [(plane, BF16)],
        [
            ((ACROSS, DOWN, 8, X), F32), ((DOWN + 8, X), F32), ((4 * X, 4 * X), BF16),
            ((X, OWN * X), BF16), ((M + 3 * DOWN, 4 * X), BF16), ((group, X), BF16),
            ((X, X), F32), (plane, BF16), pltpu.SemaphoreType.DMA((OWN,)),
        ],
        10**6,
        out_specs=in_hbm,
    )(returned.reshape(ACROSS, DOWN, 8, X), source.reshape(plane))
    return result.reshape(OWN, 1, X, X)


def solution(mesh):
    grid = Mesh(mesh.devices.reshape(-1, PLANES, OWNERS), ("x", "y", "mode"))
    placed = P("mode", ("x", "y"), None, None)
    return jax.shard_map(
        shards, mesh=grid, in_specs=(placed, placed, placed, P(), P()), out_specs=placed, check_vma=False
    )
```

time: 164 us -> 73.3 us (0.45)
  waiting for transfers between devices: 59.1 us -> 0.01 us
  starting transfers between devices: 42.5 us -> 6.49 us
  blocking collectives: 42.3 us -> 58.1 us
  matrix products: 8.06 us -> 0 us
  Pallas kernels: 0 us -> 7.89 us
  local copies, waits for them, and re-layouts: 7.86 us -> 0.33 us
  other arithmetic: 2.28 us -> 0 us
    all_to_all x5 -> x0, waiting for transfers between devices: 59.1 us -> none  [the longest x1 15 us: shards(): lax.all_to_all(log_coeffs.astype(jnp.float32), 'mode', split_axis=2, conc...]
    all_to_all x5 -> x0, starting transfers between devices: 31.7 us -> none  [the longest x1 11.7 us: shards(): lax.all_to_all(log_coeffs.astype(jnp.float32), 'mode', split_axis=2, conc...]
    all_to_all x2, blocking collectives: 42.3 us -> 58.1 us  [exchange(): lax.all_to_all(block, ('y', 'mode'), split_axis=0, concat_axis=0, tiled=T...]
    dot_general x7 -> x0, matrix products: 8.06 us -> none  [apply_matrix(): jnp.dot(matrix, flat, precision=lax.Precision.HIGHEST, preferred_element_...]
    pallas_call x0 -> x4, Pallas kernels: none -> 7.89 us  [the longest x1 3.27 us: shards(): call(own_kernel, [((Q, M), BF16), ((Q, M), BF16), ((M, Q), BF16), ((M, Q)...]
    ppermute x2, starting transfers between devices: 10.8 us -> 6.49 us  [neighbour(): return lax.ppermute(block, 'x', route)]
    dot_general x3 -> x0, local copies, waits for them, and re-layouts: 3.03 us -> none  [apply_matrix(): jnp.dot(matrix, flat, precision=lax.Precision.HIGHEST, preferred_element_...]
    convert_element_type x1 -> x0, local copies, waits for them, and re-layouts: 1.85 us -> none  [shards(): log_coeffs.astype(jnp.float32)]
  transfers between devices with their start and end apart: 7 -> 2, of which waited for: 5 -> 0; matrix products, arithmetic and copies ran while one was open for 10% -> 0% of each run, Pallas kernels for 0% -> 4%
where the time goes in v2:
time: 73.3 us; the launch traced here: 73 us
  blocking collectives  58.1 us (79%)
  Pallas kernels  7.89 us (11%)
  starting transfers between devices  6.49 us (9%)
    all_to_all x2, blocking collectives, exchange(): lax.all_to_all(block, ('y', 'mode'), split_axis=0, concat_axis=0, tiled=T...  58.1 us
    ppermute x2, starting transfers between devices, neighbour(): return lax.ppermute(block, 'x', route)  6.49 us
    pallas_call x1, Pallas kernels, shards(): call(own_kernel, [((Q, M), BF16), ((Q, M), BF16), ((M, Q), BF16), ((M, Q)...  3.27 us
    pallas_call x1, Pallas kernels, shards(): call(finish_kernel, [(plane, BF16)], [((ACROSS, DOWN, 8, X), F32), ((DOWN...  1.74 us
    pallas_call x1, Pallas kernels, shards(): call(pack_kernel, [((group * SENT, X), BF16)], [((2, *plane), BF16), ((X,...  1.73 us
  transfers between devices with their start and end apart: 2, of which 0 were waited for; matrix products, arithmetic and copies ran while one was open for 0% of the time, Pallas kernels for 4%

profile of v2, /device:TPU:1, one launch (start us, length us, event | category | flops | bytes accessed | tf_op | source)
XLA Modules:
  0.0 73.0 jit_solution(17372939816798569680)
XLA Ops:
  0.0 1.7 %shard_map.55 = bf16[1792,128]{1,0:T(8,128)(2,1)S(1)} custom-call(bf16[6,128,128]{2,1,0:T(8,128)(2,1)} %bitcast.19, bf16[6,128,128]{2,1,0:T(8,128)(2,1)} %bitcast.20), custom_call_target="tpu_custom_call" | custom-call | flops 1000000 | bytes 1048576 | tf_op jit(solution)/shard_map/pallas_call | solution.py:307
  1.7 0.0 copy-start.2
  1.7 37.0 %all_to_all.10 = bf16[128,7,2,128]{3,2,1,0:T(2,128)(2,1)S(1)} all-to-all(bf16[128,7,2,128]{3,2,1,0:T(2,128)(2,1)S(1)} %bitcast.12), channel_id=1, replica_groups=mesh['x'=4,'y'=4,'mode'=32] {'y','mode'}, dimensions={0} | all-to-all | bytes 917504 | tf_op jit(solution)/shard_map/all_to_all | solution.py:300
  38.8 0.1 slice.9
  38.9 3.1 %collective-permute-start.1 = (bf16[32,7,2,128]{3,2,1,0:T(2,128)(2,1)S(1)}, bf16[32,7,2,128]{3,2,1,0:T(2,128)(2,1)S(1)}, u32[]{:S(2)}, u32[]{:S(2)}) collective-permute-start(bf16[32,7,2,128]{3,2,1,0:T(2,128)(2,1)S(1)} %slice.9), channel_id=1, source_target_pairs={{384,0},{0,128},{128,256},{256,384},{385,1},{1,129},{129,257},{257... | collective-permute-start | bytes 344072 | tf_op jit(solution)/shard_map/ppermute | solution.py:296
  42.0 0.0 copy-done.2
  42.0 0.2 copy.6.vander_ref
  42.2 0.0 copy-start.1
  42.3 3.4 %collective-permute-start = (bf16[32,3,2,128]{3,2,1,0:T(2,128)(2,1)S(1)}, bf16[32,3,2,128]{3,2,1,0:T(2,128)(2,1)S(1)}, u32[]{:S(2)}, u32[]{:S(2)}) collective-permute-start(bf16[32,3,2,128]{3,2,1,0:T(2,128)(2,1)S(1)} %slice.8), channel_id=1, source_target_pairs={{128,0},{256,128},{384,256},{0,384},{129,1},{257,129},{385,257},{1... | collective-permute-start | bytes 147464 | tf_op jit(solution)/shard_map/ppermute | solution.py:296
  45.6 0.0 copy-done.1
  45.6 3.3 %shard_map.56 = (bf16[512,192]{1,0:T(8,128)(2,1)S(1)}, bf16[512,192]{1,0:T(8,128)(2,1)S(1)}, bf16[192,512]{1,0:T(8,128)(2,1)S(1)}, bf16[192,512]{1,0:T(8,128)(2,...) custom-call(bf16[1792,128]{1,0:T(8,128)(2,1)S(1)} %bitcast.14, ...), custom_call_target="tpu_custom_call" | custom-call | flops 1000000000 | bytes 1048576 | tf_op jit(solution)/shard_map/pallas_call | solution.py:321
  48.9 0.0 collective-permute-done
  48.9 0.0 collective-permute-done.1
  48.9 1.2 %shard_map.57 = bf16[128,8,128]{2,1,0:T(8,128)(2,1)S(1)} custom-call(bf16[192,128]{1,0:T(8,128)(2,1)S(1)} %bitcast.17, bf16[448,128]{1,0:T(8,128)(2,1)S(1)} %bitcast.16, bf16[512,192]{1,0:T(8,128)(2,1)S(1)} %get-tuple-element.12.vh_ref, bf16[512,192]{1,0:T(8,128)(2,1)S(1)} %get-tuple-element.13.vl_ref, bf16[192,512]{1,0:T(8,128)(2,1)S(1)} %get-tuple-element.14.ph_ref, ...), custom_call_target="tpu_custom_call" | custom-call | flops 1000000000 | bytes 1048576 | tf_op jit(solution)/shard_map/pallas_call | solution.py:334
  50.1 0.0 copy-start
  50.1 21.1 %all_to_all.11 = bf16[128,8,128]{2,1,0:T(8,128)(2,1)S(1)} all-to-all(bf16[128,8,128]{2,1,0:T(8,128)(2,1)S(1)} %shard_map.57), channel_id=1, replica_groups=mesh['x'=4,'y'=4,'mode'=32] {'y','mode'}, dimensions={0} | all-to-all | bytes 524288 | tf_op jit(solution)/shard_map/all_to_all | solution.py:300
  71.2 0.0 copy-done
  71.2 1.7 %shard_map.58 = bf16[6,128,128]{2,1,0:T(8,128)(2,1)} custom-call(bf16[4,32,8,128]{3,2,1,0:T(8,128)(2,1)S(1)} %bitcast.13, bf16[6,128,128]{2,1,0:T(8,128)(2,1)S(1)} %bitcast.15), custom_call_target="tpu_custom_call" | custom-call | flops 1000000 | bytes 1048576 | tf_op jit(solution)/shard_map/pallas_call | solution.py:341
  (1 shorter events, 0.0 us)
Async XLA Ops:
  1.7 40.3 %copy-start.2 = (f32[512,192]{0,1:T(8,128)S(1)}, f32[512,192]{0,1:T(8,128)}, u32[]{:S(2)}) copy-start(f32[512,192]{0,1:T(8,128)} %param.8) | copy-start | bytes 1179652
  38.9 10.1 %collective-permute-start.1 = (bf16[32,7,2,128]{3,2,1,0:T(2,128)(2,1)S(1)}, bf16[32,7,2,128]{3,2,1,0:T(2,128)(2,1)S(1)}, u32[]{:S(2)}, u32[]{:S(2)}) collective-permute-start(bf16[32,7,2,128]{3,2,1,0:T(2,128)(2,1)S(1)} %slice.9), channel_id=1, source_target_pairs={{384,0},{0,128},{128,256},{256,384},{385,1},{1,129},{129,257},{257... | collective-permute-start | bytes 344072 | tf_op jit(solution)/shard_map/ppermute | solution.py:296
  42.2 3.4 %copy-start.1 = (f32[512]{0:T(512)S(1)}, f32[512]{0:T(512)}, u32[]{:S(2)}) copy-start(f32[512]{0:T(512)} %param.9) | copy-start | bytes 6148
  42.3 6.7 %collective-permute-start = (bf16[32,3,2,128]{3,2,1,0:T(2,128)(2,1)S(1)}, bf16[32,3,2,128]{3,2,1,0:T(2,128)(2,1)S(1)}, u32[]{:S(2)}, u32[]{:S(2)}) collective-permute-start(bf16[32,3,2,128]{3,2,1,0:T(2,128)(2,1)S(1)} %slice.8), channel_id=1, source_target_pairs={{128,0},{256,128},{384,256},{0,384},{129,1},{257,129},{385,257},{1... | collective-permute-start | bytes 147464 | tf_op jit(solution)/shard_map/ppermute | solution.py:296
  50.1 21.1 %copy-start = (bf16[6,1,128,128]{3,2,1,0:T(8,128)(2,1)S(1)}, bf16[6,1,128,128]{3,2,1,0:T(8,128)(2,1)}, u32[]{:S(2)}) copy-start(bf16[6,1,128,128]{3,2,1,0:T(8,128)(2,1)} %param.7) | copy-start | bytes 589828

commit v3 on v2

--- a/solution.py
+++ b/solution.py
@@ -36,9 +36,9 @@
     return dot(vh_ref[...], field) + dot(vl_ref[...], field)
 
 
-def project(ph_ref, pl_ref, flux):
+def project(ph_ref, flux):
     fh, fl = halves(flux)
-    return dot(ph_ref[...], fh) + dot(pl_ref[...], fh) + dot(ph_ref[...], fl)
+    return dot(ph_ref[...], fh) + dot(ph_ref[...], fl)
 
 
 def lane_of(rows):
@@ -69,13 +69,49 @@
     return copies
 
 
-def pack_kernel(log_any, pressure_any, out_ref, planes, flat, ring, swap, shift, cells, heads, block, sems):
+def fill_tables(past_ref, beside_ref):
+    row, col = grid_of(X, X)
+    within = col % COLS
+    for m in range(4):
+        past_ref[:, m * X : (m + 1) * X] = select((col >= 96) & (row == col - 96 + COLS * m))
+    for m in range(OWN):
+        at = (4 + m) * X
+        past_ref[:, at : at + X] = select((within == COLS - 1) & (row == col - 5 + m))
+    for m in range(4, OWN):
+        at = (6 + m) * X
+        half = jnp.where(col >= 112, 80, 96)
+        past_ref[:, at : at + X] = select((col >= 96) & (row == col - half + 64 * (m - 4)))
+    for m in range(OWN):
+        here = select((within == 0) & (row == (col + X - COLS) % X + 26 + m))
+        beside_ref[:, m * X : (m + 1) * X] = here
+
+
+def fill_matrices(turned_ref, weights_ref, vh_ref, vl_ref, ph_ref, chunk, ordered):
+    for c in range(Q // X):
+        points = slice(c * X, (c + 1) * X)
+        chunk[...] = turned_ref[:, points]
+        for m in range(OWN):
+            ordered[m * OWNERS : (m + 1) * OWNERS, points] = chunk[pl.ds(m, OWNERS, stride=OWN), :]
+    vh_ref[...], vl_ref[...] = halves(jnp.transpose(ordered[...]))
+    ph_ref[...] = (ordered[...] * weights_ref[...]).astype(BF16)
+
+
+def pack_kernel(
+    log_any, pressure_any, turned_any, weights_any,
+    out_ref, vh_ref, vl_ref, ph_ref, past_ref, swap, beside_ref,
+    planes, flat, ring, shift, cells, heads, block, turned, weights, chunk, ordered, sems, table_sems,
+):
     copies = start_all([
         pltpu.make_async_copy(ref.at[m], planes.at[field, m], sems.at[field, m])
         for field, ref in enumerate((log_any, pressure_any))
         for m in range(OWN)
     ])
+    tables = start_all([
+        pltpu.make_async_copy(turned_any, turned, table_sems.at[0]),
+        pltpu.make_async_copy(weights_any, weights, table_sems.at[1]),
+    ])
     swap[...] = swapper()
+    fill_tables(past_ref, beside_ref)
     row, col = grid_of(X, X)
     for m in range(OWN):
         shift[m * X : (m + 1) * X, :] = select((col % COLS == 26 + m) & (row == col - 26 - m))
@@ -115,31 +151,18 @@
         total = jnp.where(within < 16, ends, rights[b * DOWN : (b + 1) * DOWN])
         block[pl.ds(SENT * DOWN * b + 7, DOWN, stride=SENT), :] = total
     out_ref[...] = block[...].astype(BF16)
+    for copy in tables:
+        copy.wait()
+    fill_matrices(turned, weights, vh_ref, vl_ref, ph_ref, chunk, ordered)
 
 
 def own_kernel(
-    got_ref, vander_ref, weights_ref,
-    vh_ref, vl_ref, ph_ref, pl_ref, factor_ref, field_ref, block_ref,
-    wide, turned, ordered, logs, press, right, below, cells, ends, edges, columns,
+    got_ref, vh_ref, vl_ref, ph_ref, columns,
+    factor_ref, field_ref, block_ref,
+    wide, logs, press, right, below, cells, ends, edges,
 ):
-    for c in range(Q // X):
-        points = slice(c * X, (c + 1) * X)
-        turned[...] = jnp.transpose(vander_ref[points, :])
-        for m in range(OWN):
-            ordered[m * OWNERS : (m + 1) * OWNERS, points] = turned[pl.ds(m, OWNERS, stride=OWN), :]
-    vh_ref[...], vl_ref[...] = halves(jnp.transpose(ordered[...]))
-    ph_ref[...], pl_ref[...] = halves(ordered[...] * weights_ref[...])
     row, col = grid_of(X, X)
     within = col % COLS
-    for m in range(4):
-        columns[:, m * X : (m + 1) * X] = select((col >= 96) & (row == col - 96 + COLS * m))
-    for m in range(OWN):
-        at = (4 + m) * X
-        columns[:, at : at + X] = select((within == COLS - 1) & (row == col - 5 + m))
-    for m in range(4, OWN):
-        at = (6 + m) * X
-        half = jnp.where(col >= 112, 80, 96)
-        columns[:, at : at + X] = select((col >= 96) & (row == col - half + 64 * (m - 4)))
     wide[...] = got_ref[...].astype(F32)
     for k in range(PLANES):
         lanes = slice(k * X, (k + 1) * X)
@@ -152,32 +175,29 @@
             logs[modes, lanes] = wide[pl.ds(SENT * OWNERS * k + m, OWNERS, stride=SENT), :].astype(BF16)
             here = wide[pl.ds(SENT * OWNERS * k + 8 + m, OWNERS, stride=SENT), :].astype(BF16)
             press[modes, lanes] = here
-            cells[k * M + m * OWNERS : k * M + (m + 1) * OWNERS, :] = here
-    next_x = dot(cells[...], select((within < COLS - 1) & (row == col + 1)))
-    next_y = dot(cells[...], select(row == col + COLS))
-    past_y = dot(ends[0], columns[:, 0 : 4 * X])
-    past = dot(ends[1], columns[:, 4 * X :])
-    for k in range(PLANES):
-        lanes = slice(k * X, (k + 1) * X)
-        owners = slice(k * OWNERS, (k + 1) * OWNERS)
-        for m in range(OWN):
-            modes = slice(m * OWNERS, (m + 1) * OWNERS)
-            rows = slice(k * M + m * OWNERS, k * M + (m + 1) * OWNERS)
-            right[modes, lanes] = (next_x[rows] + past[owners, m * X : (m + 1) * X]).astype(BF16)
-            if m < 4:
-                after = past_y[owners, m * X : (m + 1) * X]
-            else:
-                after = past[owners, (m + 2) * X : (m + 3) * X]
-            below[modes, lanes] = (next_y[rows] + after).astype(BF16)
+            cells[m, k * OWNERS : (k + 1) * OWNERS, :] = here
+    next_x = select((within < COLS - 1) & (row == col + 1))
+    next_y = select(row == col + COLS)
+    for m in range(OWN):
+        modes = slice(m * OWNERS, (m + 1) * OWNERS)
+        at = (4 + m) * X
+        to_right = dot(cells[m], next_x) + dot(ends[1], columns[:, at : at + X])
+        at = (m if m < 4 else 6 + m) * X
+        to_below = dot(cells[m], next_y) + dot(ends[m // 4], columns[:, at : at + X])
+        for k in range(PLANES):
+            lanes = slice(k * X, (k + 1) * X)
+            owners = slice(k * OWNERS, (k + 1) * OWNERS)
+            right[modes, lanes] = to_right[owners].astype(BF16)
+            below[modes, lanes] = to_below[owners].astype(BF16)
     factor_ref[...] = jnp.exp(expand(vh_ref, vl_ref, logs[...]))
-    field_ref[...] = expand(vh_ref, vl_ref, press[...])
-    flux_x = factor_ref[...] * (expand(vh_ref, vl_ref, right[...]) - field_ref[...])
-    proj_x = project(ph_ref, pl_ref, flux_x)
-    flux_y = factor_ref[...] * (expand(vh_ref, vl_ref, below[...]) - field_ref[...])
-    proj_y = project(ph_ref, pl_ref, flux_y)
+    field_ref[...] = dot(vh_ref[...], press[...])
+    flux_x = factor_ref[...] * (dot(vh_ref[...], right[...]) - field_ref[...])
+    proj_x = project(ph_ref, flux_x)
+    flux_y = factor_ref[...] * (dot(vh_ref[...], below[...]) - field_ref[...])
+    proj_y = project(ph_ref, flux_y)
     inner = CELLS - X
     flux_z = factor_ref[:, 0:inner] * (field_ref[:, X:CELLS] - field_ref[:, 0:inner])
-    proj_z = project(ph_ref, pl_ref, flux_z)
+    proj_z = project(ph_ref, flux_z)
     xh, xl = halves(proj_x)
     yh, yl = halves(proj_y)
     less_x = (row == col).astype(F32) - ((within > 0) & (row == col - 1)).astype(F32)
@@ -208,7 +228,7 @@
 
 
 def join_kernel(
-    upper_ref, lower_ref, vh_ref, vl_ref, ph_ref, pl_ref, factor_ref, field_ref, block_ref,
+    upper_ref, lower_ref, vh_ref, vl_ref, ph_ref, factor_ref, field_ref, block_ref,
     out_ref,
     wide, above, faces, block,
 ):
@@ -220,10 +240,11 @@
         faces[modes, X : 2 * X] = wide[pl.ds(m, OWNERS, stride=SENT), :].astype(BF16)
         faces[modes, 2 * X : 3 * X] = wide[pl.ds(8 + m, OWNERS, stride=SENT), :].astype(BF16)
     last = slice(CELLS - X, CELLS)
-    values = expand(vh_ref, vl_ref, faces[...])
+    values = dot(vh_ref[...], faces[...])
     top = factor_ref[:, last] * (values[:, 0:X] - field_ref[:, last])
-    bottom = jnp.exp(values[:, X : 2 * X]) * (field_ref[:, 0:X] - values[:, 2 * X : 3 * X])
-    both = project(ph_ref, pl_ref, jnp.concatenate([bottom, top], axis=1))
+    logs = values[:, X : 2 * X] + dot(vl_ref[...], faces[:, X : 2 * X])
+    bottom = jnp.exp(logs) * (field_ref[:, 0:X] - values[:, 2 * X : 3 * X])
+    both = project(ph_ref, jnp.concatenate([bottom, top], axis=1))
     block[...] = block_ref[...]
     for m in range(OWN):
         modes = slice(m * OWNERS, (m + 1) * OWNERS)
@@ -232,13 +253,7 @@
     out_ref[...] = block[...].astype(BF16)
 
 
-def finish_kernel(got_ref, source_ref, out_any, wide, ring, swap, shift, cells, ends, flat, planes, sems):
-    swap[...] = swapper()
-    row, col = grid_of(X, X)
-    within = col % COLS
-    for m in range(OWN):
-        here = select((within == 0) & (row == (col + X - COLS) % X + 26 + m))
-        shift[:, m * X : (m + 1) * X] = here
+def finish_kernel(got_ref, source_ref, swap, shift, out_any, wide, ring, cells, ends, flat, planes, sems):
     wide[...] = got_ref[...].astype(F32)
     for b in range(ACROSS):
         lanes = slice(b * X, (b + 1) * X)
@@ -304,51 +319,58 @@
     plane = (OWN, X, X)
     group = PLANES * OWNERS
     in_hbm = pl.BlockSpec(memory_space=pltpu.HBM)
-    packed = call(
+    packed, vh, vl, ph, past, swap, beside = call(
         pack_kernel,
-        [((group * SENT, X), BF16)],
+        [
+            ((group * SENT, X), BF16), ((Q, M), BF16), ((Q, M), BF16), ((M, Q), BF16),
+            ((X, 12 * X), BF16), ((4 * X, 4 * X), BF16), ((X, OWN * X), BF16),
+        ],
         [
             ((2, *plane), BF16), ((X, X), F32), ((DOWN + 8, X), F32),
-            ((4 * X, 4 * X), BF16), ((OWN * X, X), BF16), ((2 * M + 2 * DOWN, 4 * X), BF16),
-            ((ACROSS * DOWN, OWN * X), BF16), ((group * SENT, X), F32), pltpu.SemaphoreType.DMA((2, OWN)),
+            ((OWN * X, X), BF16), ((2 * M + 2 * DOWN, 4 * X), BF16),
+            ((ACROSS * DOWN, OWN * X), BF16), ((group * SENT, X), F32),
+            ((M, Q), F32), ((1, Q), F32), ((M, X), F32), ((M, Q), F32),
+            pltpu.SemaphoreType.DMA((2, OWN)), pltpu.SemaphoreType.DMA((2,)),
         ],
         10**6,
-        in_specs=[in_hbm] * 2,
-    )(*[pltpu.with_memory_space_constraint(field.reshape(plane), pltpu.HBM) for field in (log_coeffs, pressure)])
+        in_specs=[in_hbm] * 4,
+    )(*[
+        pltpu.with_memory_space_constraint(array, pltpu.HBM)
+        for array in (
+            log_coeffs.reshape(plane), pressure.reshape(plane), vandermonde.T, weights.reshape(1, Q)
+        )
+    ])
+    halved = (vh, vl, ph)
     got = exchange(packed.reshape(group, SENT // 2, 2, X))
     upper = neighbour(got[0:OWNERS, 4:7], -1).reshape(M, X)
     lower = neighbour(got[group - OWNERS : group], 1).reshape(OWNERS * SENT, X)
     own = call(
         own_kernel,
+        [((Q, CELLS), F32), ((Q, CELLS), F32), ((group, 8, X), F32)],
         [
-            ((Q, M), BF16), ((Q, M), BF16), ((M, Q), BF16), ((M, Q), BF16),
-            ((Q, CELLS), F32), ((Q, CELLS), F32), ((group, 8, X), F32),
-        ],
-        [
-            ((group * SENT, X), F32), ((M, X), F32), ((M, Q), F32),
+            ((group * SENT, X), F32),
             ((M, CELLS), BF16), ((M, CELLS), BF16), ((M, CELLS), BF16), ((M, CELLS), BF16),
-            ((PLANES * M, X), BF16), ((2, group, X), BF16), ((group, 12 * X), BF16), ((X, 12 * X), BF16),
+            ((OWN, group, X), BF16), ((2, group, X), BF16), ((group, 12 * X), BF16),
         ],
         10**9,
-    )(got.reshape(group * SENT, X), vandermonde, weights.reshape(1, Q))
+    )(got.reshape(group * SENT, X), *halved, past)
     back = call(
         join_kernel,
         [((group, 8, X), BF16)],
         [((OWNERS * SENT, X), F32), ((M, X), F32), ((M, 3 * X), BF16), ((group, 8, X), F32)],
         10**9,
-    )(upper, lower, *own)
+    )(upper, lower, *halved, *own)
     returned = exchange(back)
     result = call(
         finish_kernel,
         [(plane, BF16)],
         [
-            ((ACROSS, DOWN, 8, X), F32), ((DOWN + 8, X), F32), ((4 * X, 4 * X), BF16),
-            ((X, OWN * X), BF16), ((M + 3 * DOWN, 4 * X), BF16), ((group, X), BF16),
-            ((X, X), F32), (plane, BF16), pltpu.SemaphoreType.DMA((OWN,)),
+            ((ACROSS, DOWN, 8, X), F32), ((DOWN + 8, X), F32), ((M + 3 * DOWN, 4 * X), BF16),
+            ((group, X), BF16), ((X, X), F32), (plane, BF16), pltpu.SemaphoreType.DMA((OWN,)),
         ],
         10**6,
         out_specs=in_hbm,
-    )(returned.reshape(ACROSS, DOWN, 8, X), source.reshape(plane))
+    )(returned.reshape(ACROSS, DOWN, 8, X), source.reshape(plane), swap, beside)
     return result.reshape(OWN, 1, X, X)
 
 

time: 73.3 us -> 72 us (0.982)
  Pallas kernels: 7.89 us -> 7 us
  transfers between devices with their start and end apart: 2 -> 2, of which waited for: 0 -> 0; matrix products, arithmetic and copies ran while one was open for 0% -> 0% of each run, Pallas kernels for 4% -> 3%
where the time goes in v3:
time: 72 us; the launch traced here: 71.7 us
  blocking collectives  58 us (81%)
  Pallas kernels  7 us (10%)
  starting transfers between devices  6.49 us (9%)
    all_to_all x2, blocking collectives, exchange(): lax.all_to_all(block, ('y', 'mode'), split_axis=0, concat_axis=0, tiled=T...  58 us
    ppermute x2, starting transfers between devices, neighbour(): return lax.ppermute(block, 'x', route)  6.49 us
    pallas_call x1, Pallas kernels, shards(): call(own_kernel, [((Q, CELLS), F32), ((Q, CELLS), F32), ((group, 8, X), F...  2.39 us
    pallas_call x1, Pallas kernels, shards(): call(pack_kernel, [((group * SENT, X), BF16), ((Q, M), BF16), ((Q, M), BF...  2.01 us
    pallas_call x1, Pallas kernels, shards(): call(finish_kernel, [(plane, BF16)], [((ACROSS, DOWN, 8, X), F32), ((DOWN...  1.65 us
  transfers between devices with their start and end apart: 2, of which 0 were waited for; matrix products, arithmetic and copies ran while one was open for 0% of the time, Pallas kernels for 3%

profile of v3, /device:TPU:1, one launch (start us, length us, event | category | flops | bytes accessed | tf_op | source)
XLA Modules:
  0.0 71.7 jit_solution(7125406300986014547)
XLA Ops:
  0.0 2.0 %shard_map.55 = (bf16[1792,128]{1,0:T(8,128)(2,1)S(1)}, bf16[512,192]{1,0:T(8,128)(2,1)S(1)}, bf16[512,192]{1,0:T(8,128)(2,1)S(1)}, bf16[192,512]{1,0:T(8,128)(2...) custom-call(bf16[6,128,128]{2,1,0:T(8,128)(2,1)} %bitcast.20, ...), custom_call_target="tpu_custom_call" | custom-call | flops 1000000 | bytes 1048576 | tf_op jit(solution)/shard_map/pallas_call | solution.py:322
  2.0 36.9 %all_to_all.10 = bf16[128,7,2,128]{3,2,1,0:T(2,128)(2,1)S(1)} all-to-all(bf16[128,7,2,128]{3,2,1,0:T(2,128)(2,1)S(1)} %bitcast.15), channel_id=1, replica_groups=mesh['x'=4,'y'=4,'mode'=32] {'y','mode'}, dimensions={0} | all-to-all | bytes 917504 | tf_op jit(solution)/shard_map/all_to_all | solution.py:315
  38.9 0.1 slice.9
  39.0 3.1 %collective-permute-start.1 = (bf16[32,7,2,128]{3,2,1,0:T(2,128)(2,1)S(1)}, bf16[32,7,2,128]{3,2,1,0:T(2,128)(2,1)S(1)}, u32[]{:S(2)}, u32[]{:S(2)}) collective-permute-start(bf16[32,7,2,128]{3,2,1,0:T(2,128)(2,1)S(1)} %slice.9), channel_id=1, source_target_pairs={{384,0},{0,128},{128,256},{256,384},{385,1},{1,129},{129,257},{257... | collective-permute-start | bytes 344072 | tf_op jit(solution)/shard_map/ppermute | solution.py:311
  42.2 3.4 %collective-permute-start = (bf16[32,3,2,128]{3,2,1,0:T(2,128)(2,1)S(1)}, bf16[32,3,2,128]{3,2,1,0:T(2,128)(2,1)S(1)}, u32[]{:S(2)}, u32[]{:S(2)}) collective-permute-start(bf16[32,3,2,128]{3,2,1,0:T(2,128)(2,1)S(1)} %slice.8), channel_id=1, source_target_pairs={{128,0},{256,128},{384,256},{0,384},{129,1},{257,129},{385,257},{1... | collective-permute-start | bytes 147464 | tf_op jit(solution)/shard_map/ppermute | solution.py:311
  45.6 2.4 %shard_map.56 = (f32[512,512]{1,0:T(8,128)S(1)}, f32[512,512]{1,0:T(8,128)S(1)}, f32[128,8,128]{2,1,0:T(8,128)S(1)}) custom-call(bf16[1792,128]{1,0:T(8,128)(2,1)S(1)} %bitcast.14, bf16[512,192]{1,0:T(8,128)(2,1)S(1)} %get-tuple-element.16.vh_ref, bf16[512,192]{1,0:T(8,128)(2,1)S(1)} %get-tuple-element.17.vl_ref, ...), custom_call_target="tpu_custom_call" | custom-call | flops 1000000000 | bytes 1048576 | tf_op jit(solution)/shard_map/pallas_call | solution.py:347
  48.0 0.0 collective-permute-done
  48.0 0.0 collective-permute-done.1
  48.0 0.9 %shard_map.57 = bf16[128,8,128]{2,1,0:T(8,128)(2,1)S(1)} custom-call(bf16[192,128]{1,0:T(8,128)(2,1)S(1)} %bitcast.18, bf16[448,128]{1,0:T(8,128)(2,1)S(1)} %bitcast.17, bf16[512,192]{1,0:T(8,128)(2,1)S(1)} %get-tuple-element.16.vh_ref, bf16[512,192]{1,0:T(8,128)(2,1)S(1)} %get-tuple-element.17.vl_ref, bf16[192,512]{1,0:T(8,128)(2,1)S(1)} %get-tuple-element.18.ph_ref, ...), custom_call_target="tpu_custom_call" | custom-call | flops 1000000000 | bytes 1048576 | tf_op jit(solution)/shard_map/pallas_call | solution.py:357
  48.9 0.0 copy-start
  48.9 21.1 %all_to_all.11 = bf16[128,8,128]{2,1,0:T(8,128)(2,1)S(1)} all-to-all(bf16[128,8,128]{2,1,0:T(8,128)(2,1)S(1)} %shard_map.57), channel_id=1, replica_groups=mesh['x'=4,'y'=4,'mode'=32] {'y','mode'}, dimensions={0} | all-to-all | bytes 524288 | tf_op jit(solution)/shard_map/all_to_all | solution.py:315
  70.1 0.0 copy-done
  70.1 1.7 %shard_map.58 = bf16[6,128,128]{2,1,0:T(8,128)(2,1)} custom-call(bf16[4,32,8,128]{3,2,1,0:T(8,128)(2,1)S(1)} %bitcast.13, bf16[6,128,128]{2,1,0:T(8,128)(2,1)S(1)} %bitcast.16, bf16[512,512]{1,0:T(8,128)(2,1)S(1)} %get-tuple-element.23.swap, bf16[128,768]{1,0:T(8,128)(2,1)S(1)} %get-tuple-element.24.shift), custom_call_target="tpu_custom_call" | custom-call | flops 1000000 | bytes 1048576 | tf_op jit(solution)/shard_map/pallas_call | solution.py:364
  (1 shorter events, 0.0 us)
Async XLA Ops:
  39.0 9.0 %collective-permute-start.1 = (bf16[32,7,2,128]{3,2,1,0:T(2,128)(2,1)S(1)}, bf16[32,7,2,128]{3,2,1,0:T(2,128)(2,1)S(1)}, u32[]{:S(2)}, u32[]{:S(2)}) collective-permute-start(bf16[32,7,2,128]{3,2,1,0:T(2,128)(2,1)S(1)} %slice.9), channel_id=1, source_target_pairs={{384,0},{0,128},{128,256},{256,384},{385,1},{1,129},{129,257},{257... | collective-permute-start | bytes 344072 | tf_op jit(solution)/shard_map/ppermute | solution.py:311
  42.2 5.8 %collective-permute-start = (bf16[32,3,2,128]{3,2,1,0:T(2,128)(2,1)S(1)}, bf16[32,3,2,128]{3,2,1,0:T(2,128)(2,1)S(1)}, u32[]{:S(2)}, u32[]{:S(2)}) collective-permute-start(bf16[32,3,2,128]{3,2,1,0:T(2,128)(2,1)S(1)} %slice.8), channel_id=1, source_target_pairs={{128,0},{256,128},{384,256},{0,384},{129,1},{257,129},{385,257},{1... | collective-permute-start | bytes 147464 | tf_op jit(solution)/shard_map/ppermute | solution.py:311
  48.9 21.1 %copy-start = (bf16[6,1,128,128]{3,2,1,0:T(8,128)(2,1)S(1)}, bf16[6,1,128,128]{3,2,1,0:T(8,128)(2,1)}, u32[]{:S(2)}) copy-start(bf16[6,1,128,128]{3,2,1,0:T(8,128)(2,1)} %param.7) | copy-start | bytes 589828

commit v4 on v3

--- a/solution.py
+++ b/solution.py
@@ -89,7 +89,7 @@
 def fill_matrices(turned_ref, weights_ref, vh_ref, vl_ref, ph_ref, chunk, ordered):
     for c in range(Q // X):
         points = slice(c * X, (c + 1) * X)
-        chunk[...] = turned_ref[:, points]
+        chunk[0:M] = turned_ref[:, points]
         for m in range(OWN):
             ordered[m * OWNERS : (m + 1) * OWNERS, points] = chunk[pl.ds(m, OWNERS, stride=OWN), :]
     vh_ref[...], vl_ref[...] = halves(jnp.transpose(ordered[...]))
@@ -118,7 +118,7 @@
     for field in range(2):
         for m in range(OWN):
             copies[field * OWN + m].wait()
-            flat[...] = planes[field, m].astype(F32)
+            flat[0:X] = planes[field, m].astype(F32)
             rows = slice((field * OWN + m) * DOWN, (field * OWN + m + 1) * DOWN)
             for j in range(ROWS):
                 cells[rows, j * X : (j + 1) * X] = flat[pl.ds(j, DOWN, stride=ROWS), :].astype(BF16)
@@ -135,7 +135,7 @@
     swapped = dot(cells[...], swap[...])
     for b in range(ACROSS):
         start = SENT * DOWN * b
-        for field, offset in enumerate((0, 8)):
+        for field, offset in enumerate((0, OWN)):
             for m in range(OWN):
                 rows = slice((field * OWN + m) * DOWN, (field * OWN + m + 1) * DOWN)
                 total = swapped[rows, b * X : (b + 1) * X]
@@ -143,14 +143,14 @@
                 if field:
                     left = (b - 1) % ACROSS
                     heads[left * DOWN : (left + 1) * DOWN, m * X : (m + 1) * X] = total.astype(BF16)
-        block[pl.ds(start + 6, DOWN, stride=SENT), :] = swapped[2 * M : 2 * M + DOWN, b * X : (b + 1) * X]
+        block[pl.ds(start + 12, DOWN, stride=SENT), :] = swapped[2 * M : 2 * M + DOWN, b * X : (b + 1) * X]
     rights = dot(heads[...], shift[...])
     within = lane_of(DOWN) % COLS
     for b in range(ACROSS):
         ends = swapped[2 * M + DOWN :, b * X : (b + 1) * X]
         total = jnp.where(within < 16, ends, rights[b * DOWN : (b + 1) * DOWN])
-        block[pl.ds(SENT * DOWN * b + 7, DOWN, stride=SENT), :] = total
-    out_ref[...] = block[...].astype(BF16)
+        block[pl.ds(SENT * DOWN * b + 13, DOWN, stride=SENT), :] = total
+    out_ref[...] = block[0 : out_ref.shape[0]].astype(BF16)
     for copy in tables:
         copy.wait()
     fill_matrices(turned, weights, vh_ref, vl_ref, ph_ref, chunk, ordered)
@@ -163,17 +163,17 @@
 ):
     row, col = grid_of(X, X)
     within = col % COLS
-    wide[...] = got_ref[...].astype(F32)
+    wide[0 : got_ref.shape[0]] = got_ref[...].astype(F32)
     for k in range(PLANES):
         lanes = slice(k * X, (k + 1) * X)
         for r in range(2):
             ends[r, k * OWNERS : (k + 1) * OWNERS, :] = wide[
-                pl.ds(SENT * OWNERS * k + 6 + r, OWNERS, stride=SENT), :
+                pl.ds(SENT * OWNERS * k + 12 + r, OWNERS, stride=SENT), :
             ].astype(BF16)
         for m in range(OWN):
             modes = slice(m * OWNERS, (m + 1) * OWNERS)
             logs[modes, lanes] = wide[pl.ds(SENT * OWNERS * k + m, OWNERS, stride=SENT), :].astype(BF16)
-            here = wide[pl.ds(SENT * OWNERS * k + 8 + m, OWNERS, stride=SENT), :].astype(BF16)
+            here = wide[pl.ds(SENT * OWNERS * k + 6 + m, OWNERS, stride=SENT), :].astype(BF16)
             press[modes, lanes] = here
             cells[m, k * OWNERS : (k + 1) * OWNERS, :] = here
     next_x = select((within < COLS - 1) & (row == col + 1))
@@ -232,13 +232,13 @@
     out_ref,
     wide, above, faces, block,
 ):
-    above[...] = upper_ref[...].astype(F32)
-    wide[...] = lower_ref[...].astype(F32)
+    above[0:M] = upper_ref[...].astype(F32)
+    wide[0 : 2 * M] = lower_ref[...].astype(F32)
     for m in range(OWN):
         modes = slice(m * OWNERS, (m + 1) * OWNERS)
         faces[modes, 0:X] = above[pl.ds(m, OWNERS, stride=OWN), :].astype(BF16)
-        faces[modes, X : 2 * X] = wide[pl.ds(m, OWNERS, stride=SENT), :].astype(BF16)
-        faces[modes, 2 * X : 3 * X] = wide[pl.ds(8 + m, OWNERS, stride=SENT), :].astype(BF16)
+        faces[modes, X : 2 * X] = wide[pl.ds(m, OWNERS, stride=2 * OWN), :].astype(BF16)
+        faces[modes, 2 * X : 3 * X] = wide[pl.ds(OWN + m, OWNERS, stride=2 * OWN), :].astype(BF16)
     last = slice(CELLS - X, CELLS)
     values = dot(vh_ref[...], faces[...])
     top = factor_ref[:, last] * (values[:, 0:X] - field_ref[:, last])
@@ -285,7 +285,7 @@
                 far = turn(halved[:, at + X : at + 2 * X], 16)
                 total = total - jnp.where(inside, halved[:, at : at + X], far)
             flat[pl.ds(j, DOWN, stride=ROWS), :] = total
-        planes[m] = (-flat[...] - source_ref[m].astype(F32)).astype(BF16)
+        planes[m] = (-flat[0:X] - source_ref[m].astype(F32)).astype(BF16)
         copies.append(pltpu.make_async_copy(planes.at[m], out_any.at[m], sems.at[m]))
         copies[m].start()
     for copy in copies:
@@ -326,10 +326,10 @@
             ((X, 12 * X), BF16), ((4 * X, 4 * X), BF16), ((X, OWN * X), BF16),
         ],
         [
-            ((2, *plane), BF16), ((X, X), F32), ((DOWN + 8, X), F32),
+            ((2, *plane), BF16), ((X + 8, X), F32), ((DOWN + 8, X), F32),
             ((OWN * X, X), BF16), ((2 * M + 2 * DOWN, 4 * X), BF16),
-            ((ACROSS * DOWN, OWN * X), BF16), ((group * SENT, X), F32),
-            ((M, Q), F32), ((1, Q), F32), ((M, X), F32), ((M, Q), F32),
+            ((ACROSS * DOWN, OWN * X), BF16), ((group * SENT + 16, X), F32),
+            ((M, Q), F32), ((1, Q), F32), ((M + 8, X), F32), ((M, Q), F32),
             pltpu.SemaphoreType.DMA((2, OWN)), pltpu.SemaphoreType.DMA((2,)),
         ],
         10**6,
@@ -342,13 +342,13 @@
     ])
     halved = (vh, vl, ph)
     got = exchange(packed.reshape(group, SENT // 2, 2, X))
-    upper = neighbour(got[0:OWNERS, 4:7], -1).reshape(M, X)
-    lower = neighbour(got[group - OWNERS : group], 1).reshape(OWNERS * SENT, X)
+    upper = neighbour(got[0:OWNERS, 3:6], -1).reshape(M, X)
+    lower = neighbour(got[group - OWNERS : group, 0:6], 1).reshape(2 * M, X)
     own = call(
         own_kernel,
         [((Q, CELLS), F32), ((Q, CELLS), F32), ((group, 8, X), F32)],
         [
-            ((group * SENT, X), F32),
+            ((group * SENT + 16, X), F32),
             ((M, CELLS), BF16), ((M, CELLS), BF16), ((M, CELLS), BF16), ((M, CELLS), BF16),
             ((OWN, group, X), BF16), ((2, group, X), BF16), ((group, 12 * X), BF16),
         ],
@@ -357,7 +357,7 @@
     back = call(
         join_kernel,
         [((group, 8, X), BF16)],
-        [((OWNERS * SENT, X), F32), ((M, X), F32), ((M, 3 * X), BF16), ((group, 8, X), F32)],
+        [((2 * M + 16, X), F32), ((M + 8, X), F32), ((M, 3 * X), BF16), ((group, 8, X), F32)],
         10**9,
     )(upper, lower, *halved, *own)
     returned = exchange(back)
@@ -366,7 +366,7 @@
         [(plane, BF16)],
         [
             ((ACROSS, DOWN, 8, X), F32), ((DOWN + 8, X), F32), ((M + 3 * DOWN, 4 * X), BF16),
-            ((group, X), BF16), ((X, X), F32), (plane, BF16), pltpu.SemaphoreType.DMA((OWN,)),
+            ((group, X), BF16), ((X + 8, X), F32), (plane, BF16), pltpu.SemaphoreType.DMA((OWN,)),
         ],
         10**6,
         out_specs=in_hbm,

time: 72 us -> 71.9 us (level)
  no operation moved by 1% of the time
where the time goes in v4:
time: 71.9 us; the launch traced here: 71.7 us
  blocking collectives  58 us (81%)
  Pallas kernels  6.98 us (10%)
  starting transfers between devices  6.49 us (9%)
    all_to_all x2, blocking collectives, exchange(): lax.all_to_all(block, ('y', 'mode'), split_axis=0, concat_axis=0, tiled=T...  58 us
    ppermute x2, starting transfers between devices, neighbour(): return lax.ppermute(block, 'x', route)  6.49 us
    pallas_call x1, Pallas kernels, shards(): call(own_kernel, [((Q, CELLS), F32), ((Q, CELLS), F32), ((group, 8, X), F...  2.39 us
    pallas_call x1, Pallas kernels, shards(): call(pack_kernel, [((group * SENT, X), BF16), ((Q, M), BF16), ((Q, M), BF...  2 us
    pallas_call x1, Pallas kernels, shards(): call(finish_kernel, [(plane, BF16)], [((ACROSS, DOWN, 8, X), F32), ((DOWN...  1.65 us
  transfers between devices with their start and end apart: 2, of which 0 were waited for; matrix products, arithmetic and copies ran while one was open for 0% of the time, Pallas kernels for 3%

profile of v4, /device:TPU:1, one launch (start us, length us, event | category | flops | bytes accessed | tf_op | source)
XLA Modules:
  0.0 71.7 jit_solution(16495446671442450632)
XLA Ops:
  0.0 2.0 %shard_map.55 = (bf16[1792,128]{1,0:T(8,128)(2,1)S(1)}, bf16[512,192]{1,0:T(8,128)(2,1)S(1)}, bf16[512,192]{1,0:T(8,128)(2,1)S(1)}, bf16[192,512]{1,0:T(8,128)(2...) custom-call(bf16[6,128,128]{2,1,0:T(8,128)(2,1)} %bitcast.20, ...), custom_call_target="tpu_custom_call" | custom-call | flops 1000000 | bytes 1048576 | tf_op jit(solution)/shard_map/pallas_call | solution.py:322
  2.0 36.9 %all_to_all.10 = bf16[128,7,2,128]{3,2,1,0:T(2,128)(2,1)S(1)} all-to-all(bf16[128,7,2,128]{3,2,1,0:T(2,128)(2,1)S(1)} %bitcast.15), channel_id=1, replica_groups=mesh['x'=4,'y'=4,'mode'=32] {'y','mode'}, dimensions={0} | all-to-all | bytes 917504 | tf_op jit(solution)/shard_map/all_to_all | solution.py:315
  38.9 0.1 slice.9
  39.0 3.1 %collective-permute-start.1 = (bf16[32,6,2,128]{3,2,1,0:T(2,128)(2,1)S(1)}, bf16[32,6,2,128]{3,2,1,0:T(2,128)(2,1)S(1)}, u32[]{:S(2)}, u32[]{:S(2)}) collective-permute-start(bf16[32,6,2,128]{3,2,1,0:T(2,128)(2,1)S(1)} %slice.9), channel_id=1, source_target_pairs={{384,0},{0,128},{128,256},{256,384},{385,1},{1,129},{129,257},{257... | collective-permute-start | bytes 294920 | tf_op jit(solution)/shard_map/ppermute | solution.py:311
  42.2 3.4 %collective-permute-start = (bf16[32,3,2,128]{3,2,1,0:T(2,128)(2,1)S(1)}, bf16[32,3,2,128]{3,2,1,0:T(2,128)(2,1)S(1)}, u32[]{:S(2)}, u32[]{:S(2)}) collective-permute-start(bf16[32,3,2,128]{3,2,1,0:T(2,128)(2,1)S(1)} %slice.8), channel_id=1, source_target_pairs={{128,0},{256,128},{384,256},{0,384},{129,1},{257,129},{385,257},{1... | collective-permute-start | bytes 147464 | tf_op jit(solution)/shard_map/ppermute | solution.py:311
  45.5 2.4 %shard_map.56 = (f32[512,512]{1,0:T(8,128)S(1)}, f32[512,512]{1,0:T(8,128)S(1)}, f32[128,8,128]{2,1,0:T(8,128)S(1)}) custom-call(bf16[1792,128]{1,0:T(8,128)(2,1)S(1)} %bitcast.14, bf16[512,192]{1,0:T(8,128)(2,1)S(1)} %get-tuple-element.16.vh_ref, bf16[512,192]{1,0:T(8,128)(2,1)S(1)} %get-tuple-element.17.vl_ref, ...), custom_call_target="tpu_custom_call" | custom-call | flops 1000000000 | bytes 1048576 | tf_op jit(solution)/shard_map/pallas_call | solution.py:347
  47.9 0.0 collective-permute-done
  47.9 0.0 collective-permute-done.1
  47.9 0.9 %shard_map.57 = bf16[128,8,128]{2,1,0:T(8,128)(2,1)S(1)} custom-call(bf16[192,128]{1,0:T(8,128)(2,1)S(1)} %bitcast.18, bf16[384,128]{1,0:T(8,128)(2,1)S(1)} %bitcast.17, bf16[512,192]{1,0:T(8,128)(2,1)S(1)} %get-tuple-element.16.vh_ref, bf16[512,192]{1,0:T(8,128)(2,1)S(1)} %get-tuple-element.17.vl_ref, bf16[192,512]{1,0:T(8,128)(2,1)S(1)} %get-tuple-element.18.ph_ref, ...), custom_call_target="tpu_custom_call" | custom-call | flops 1000000000 | bytes 1048576 | tf_op jit(solution)/shard_map/pallas_call | solution.py:357
  48.9 0.0 copy-start
  48.9 21.1 %all_to_all.11 = bf16[128,8,128]{2,1,0:T(8,128)(2,1)S(1)} all-to-all(bf16[128,8,128]{2,1,0:T(8,128)(2,1)S(1)} %shard_map.57), channel_id=1, replica_groups=mesh['x'=4,'y'=4,'mode'=32] {'y','mode'}, dimensions={0} | all-to-all | bytes 524288 | tf_op jit(solution)/shard_map/all_to_all | solution.py:315
  70.0 0.0 copy-done
  70.0 1.7 %shard_map.58 = bf16[6,128,128]{2,1,0:T(8,128)(2,1)} custom-call(bf16[4,32,8,128]{3,2,1,0:T(8,128)(2,1)S(1)} %bitcast.13, bf16[6,128,128]{2,1,0:T(8,128)(2,1)S(1)} %bitcast.16, bf16[512,512]{1,0:T(8,128)(2,1)S(1)} %get-tuple-element.23.swap, bf16[128,768]{1,0:T(8,128)(2,1)S(1)} %get-tuple-element.24.shift), custom_call_target="tpu_custom_call" | custom-call | flops 1000000 | bytes 1048576 | tf_op jit(solution)/shard_map/pallas_call | solution.py:364
  (1 shorter events, 0.0 us)
Async XLA Ops:
  39.0 9.0 %collective-permute-start.1 = (bf16[32,6,2,128]{3,2,1,0:T(2,128)(2,1)S(1)}, bf16[32,6,2,128]{3,2,1,0:T(2,128)(2,1)S(1)}, u32[]{:S(2)}, u32[]{:S(2)}) collective-permute-start(bf16[32,6,2,128]{3,2,1,0:T(2,128)(2,1)S(1)} %slice.9), channel_id=1, source_target_pairs={{384,0},{0,128},{128,256},{256,384},{385,1},{1,129},{129,257},{257... | collective-permute-start | bytes 294920 | tf_op jit(solution)/shard_map/ppermute | solution.py:311
  42.2 5.8 %collective-permute-start = (bf16[32,3,2,128]{3,2,1,0:T(2,128)(2,1)S(1)}, bf16[32,3,2,128]{3,2,1,0:T(2,128)(2,1)S(1)}, u32[]{:S(2)}, u32[]{:S(2)}) collective-permute-start(bf16[32,3,2,128]{3,2,1,0:T(2,128)(2,1)S(1)} %slice.8), channel_id=1, source_target_pairs={{128,0},{256,128},{384,256},{0,384},{129,1},{257,129},{385,257},{1... | collective-permute-start | bytes 147464 | tf_op jit(solution)/shard_map/ppermute | solution.py:311
  48.9 21.1 %copy-start = (bf16[6,1,128,128]{3,2,1,0:T(8,128)(2,1)S(1)}, bf16[6,1,128,128]{3,2,1,0:T(8,128)(2,1)}, u32[]{:S(2)}) copy-start(bf16[6,1,128,128]{3,2,1,0:T(8,128)(2,1)} %param.7) | copy-start | bytes 589828

commit v5 on v4

--- a/solution.py
+++ b/solution.py
@@ -97,19 +97,17 @@
 
 
 def pack_kernel(
-    log_any, pressure_any, turned_any, weights_any,
-    out_ref, vh_ref, vl_ref, ph_ref, past_ref, swap, beside_ref,
-    planes, flat, ring, shift, cells, heads, block, turned, weights, chunk, ordered, sems, table_sems,
+    log_any, pressure_any, weights_any,
+    out_ref, weights_ref, past_ref, swap, beside_ref,
+    planes, flat, ring, shift, cells, heads, block, sems, weights_sem,
 ):
     copies = start_all([
         pltpu.make_async_copy(ref.at[m], planes.at[field, m], sems.at[field, m])
         for field, ref in enumerate((log_any, pressure_any))
         for m in range(OWN)
     ])
-    tables = start_all([
-        pltpu.make_async_copy(turned_any, turned, table_sems.at[0]),
-        pltpu.make_async_copy(weights_any, weights, table_sems.at[1]),
-    ])
+    moved = pltpu.make_async_copy(weights_any, weights_ref, weights_sem)
+    moved.start()
     swap[...] = swapper()
     fill_tables(past_ref, beside_ref)
     row, col = grid_of(X, X)
@@ -151,16 +149,15 @@
         total = jnp.where(within < 16, ends, rights[b * DOWN : (b + 1) * DOWN])
         block[pl.ds(SENT * DOWN * b + 13, DOWN, stride=SENT), :] = total
     out_ref[...] = block[0 : out_ref.shape[0]].astype(BF16)
-    for copy in tables:
-        copy.wait()
-    fill_matrices(turned, weights, vh_ref, vl_ref, ph_ref, chunk, ordered)
+    moved.wait()
 
 
 def own_kernel(
-    got_ref, vh_ref, vl_ref, ph_ref, columns,
-    factor_ref, field_ref, block_ref,
-    wide, logs, press, right, below, cells, ends, edges,
+    got_ref, turned_ref, weights_ref, columns,
+    vh_ref, vl_ref, ph_ref, factor_ref, field_ref, block_ref,
+    wide, logs, press, right, below, cells, ends, edges, chunk, ordered,
 ):
+    fill_matrices(turned_ref, weights_ref, vh_ref, vl_ref, ph_ref, chunk, ordered)
     row, col = grid_of(X, X)
     within = col % COLS
     wide[0 : got_ref.shape[0]] = got_ref[...].astype(F32)
@@ -319,47 +316,47 @@
     plane = (OWN, X, X)
     group = PLANES * OWNERS
     in_hbm = pl.BlockSpec(memory_space=pltpu.HBM)
-    packed, vh, vl, ph, past, swap, beside = call(
+    packed, points, past, swap, beside = call(
         pack_kernel,
         [
-            ((group * SENT, X), BF16), ((Q, M), BF16), ((Q, M), BF16), ((M, Q), BF16),
+            ((group * SENT, X), BF16), ((1, Q), F32),
             ((X, 12 * X), BF16), ((4 * X, 4 * X), BF16), ((X, OWN * X), BF16),
         ],
         [
             ((2, *plane), BF16), ((X + 8, X), F32), ((DOWN + 8, X), F32),
             ((OWN * X, X), BF16), ((2 * M + 2 * DOWN, 4 * X), BF16),
             ((ACROSS * DOWN, OWN * X), BF16), ((group * SENT + 16, X), F32),
-            ((M, Q), F32), ((1, Q), F32), ((M + 8, X), F32), ((M, Q), F32),
-            pltpu.SemaphoreType.DMA((2, OWN)), pltpu.SemaphoreType.DMA((2,)),
+            pltpu.SemaphoreType.DMA((2, OWN)), pltpu.SemaphoreType.DMA,
         ],
         10**6,
-        in_specs=[in_hbm] * 4,
+        in_specs=[in_hbm] * 3,
     )(*[
         pltpu.with_memory_space_constraint(array, pltpu.HBM)
-        for array in (
-            log_coeffs.reshape(plane), pressure.reshape(plane), vandermonde.T, weights.reshape(1, Q)
-        )
+        for array in (log_coeffs.reshape(plane), pressure.reshape(plane), weights.reshape(1, Q))
     ])
-    halved = (vh, vl, ph)
     got = exchange(packed.reshape(group, SENT // 2, 2, X))
     upper = neighbour(got[0:OWNERS, 3:6], -1).reshape(M, X)
     lower = neighbour(got[group - OWNERS : group, 0:6], 1).reshape(2 * M, X)
     own = call(
         own_kernel,
-        [((Q, CELLS), F32), ((Q, CELLS), F32), ((group, 8, X), F32)],
+        [
+            ((Q, M), BF16), ((Q, M), BF16), ((M, Q), BF16),
+            ((Q, CELLS), F32), ((Q, CELLS), F32), ((group, 8, X), F32),
+        ],
         [
             ((group * SENT + 16, X), F32),
             ((M, CELLS), BF16), ((M, CELLS), BF16), ((M, CELLS), BF16), ((M, CELLS), BF16),
             ((OWN, group, X), BF16), ((2, group, X), BF16), ((group, 12 * X), BF16),
+            ((M + 8, X), F32), ((M, Q), F32),
         ],
         10**9,
-    )(got.reshape(group * SENT, X), *halved, past)
+    )(got.reshape(group * SENT, X), vandermonde.T, points, past)
     back = call(
         join_kernel,
         [((group, 8, X), BF16)],
         [((2 * M + 16, X), F32), ((M + 8, X), F32), ((M, 3 * X), BF16), ((group, 8, X), F32)],
         10**9,
-    )(upper, lower, *halved, *own)
+    )(upper, lower, *own)
     returned = exchange(back)
     result = call(
         finish_kernel,

time: 71.9 us -> 72 us (level)
  transfers between devices with their start and end apart: 2 -> 2, of which waited for: 0 -> 0; matrix products, arithmetic and copies ran while one was open for 0% -> 0% of each run, Pallas kernels for 3% -> 4%
where the time goes in v5:
time: 72 us; the launch traced here: 71.7 us
  blocking collectives  58.2 us (81%)
  Pallas kernels  6.85 us (10%)
  starting transfers between devices  6.49 us (9%)
    all_to_all x2, blocking collectives, exchange(): lax.all_to_all(block, ('y', 'mode'), split_axis=0, concat_axis=0, tiled=T...  58.2 us
    ppermute x2, starting transfers between devices, neighbour(): return lax.ppermute(block, 'x', route)  6.49 us
    pallas_call x1, Pallas kernels, shards(): call(own_kernel, [((Q, M), BF16), ((Q, M), BF16), ((M, Q), BF16), ((Q, CE...  2.51 us
    pallas_call x1, Pallas kernels, shards(): call(pack_kernel, [((group * SENT, X), BF16), ((1, Q), F32), ((X, 12 * X)...  1.74 us
    pallas_call x1, Pallas kernels, shards(): call(finish_kernel, [(plane, BF16)], [((ACROSS, DOWN, 8, X), F32), ((DOWN...  1.66 us
  transfers between devices with their start and end apart: 2, of which 0 were waited for; matrix products, arithmetic and copies ran while one was open for 0% of the time, Pallas kernels for 4%

profile of v5, /device:TPU:1, one launch (start us, length us, event | category | flops | bytes accessed | tf_op | source)
XLA Modules:
  0.0 71.7 jit_solution(4930779262901084877)
XLA Ops:
  0.0 1.7 %shard_map.55 = (bf16[1792,128]{1,0:T(8,128)(2,1)S(1)}, f32[1,512]{1,0:T(1,128)S(1)}, bf16[128,1536]{1,0:T(8,128)(2,1)S(1)}, bf16[512,512]{1,0:T(8,128)(2,1)S(1)}, bf16[128,768]{1,0:T(8,128)(2,1)S(1)}) custom-call(bf16[6,128,128]{2,1,0:T(8,128)(2,1)} %bitcast.20, bf16[6,128,128]{2,1,0:T(8,128)(2,1)} %bitcast.21, f32[1,512]{1,0:T(1,128)} %bitcast.22), custom_call_target="tpu_custom_call" | custom-call | flops 1000000 | bytes 1048576 | tf_op jit(solution)/shard_map/pallas_call | solution.py:319
  1.7 0.0 copy-start.1
  1.8 37.0 %all_to_all.10 = bf16[128,7,2,128]{3,2,1,0:T(2,128)(2,1)S(1)} all-to-all(bf16[128,7,2,128]{3,2,1,0:T(2,128)(2,1)S(1)} %bitcast.15), channel_id=1, replica_groups=mesh['x'=4,'y'=4,'mode'=32] {'y','mode'}, dimensions={0} | all-to-all | bytes 917504 | tf_op jit(solution)/shard_map/all_to_all | solution.py:312
  38.8 0.1 slice.9
  38.9 3.1 %collective-permute-start.1 = (bf16[32,6,2,128]{3,2,1,0:T(2,128)(2,1)S(1)}, bf16[32,6,2,128]{3,2,1,0:T(2,128)(2,1)S(1)}, u32[]{:S(2)}, u32[]{:S(2)}) collective-permute-start(bf16[32,6,2,128]{3,2,1,0:T(2,128)(2,1)S(1)} %slice.9), channel_id=1, source_target_pairs={{384,0},{0,128},{128,256},{256,384},{385,1},{1,129},{129,257},{257... | collective-permute-start | bytes 294920 | tf_op jit(solution)/shard_map/ppermute | solution.py:308
  42.0 3.4 %collective-permute-start = (bf16[32,3,2,128]{3,2,1,0:T(2,128)(2,1)S(1)}, bf16[32,3,2,128]{3,2,1,0:T(2,128)(2,1)S(1)}, u32[]{:S(2)}, u32[]{:S(2)}) collective-permute-start(bf16[32,3,2,128]{3,2,1,0:T(2,128)(2,1)S(1)} %slice.8), channel_id=1, source_target_pairs={{128,0},{256,128},{384,256},{0,384},{129,1},{257,129},{385,257},{1... | collective-permute-start | bytes 147464 | tf_op jit(solution)/shard_map/ppermute | solution.py:308
  45.4 0.0 copy-done.1
  45.4 2.5 %shard_map.56 = (bf16[512,192]{1,0:T(8,128)(2,1)S(1)}, bf16[512,192]{1,0:T(8,128)(2,1)S(1)}, bf16[192,512]{1,0:T(8,128)(2,1)S(1)}, f32[512,512]{1,0:T(8,128)S(1)...) custom-call(bf16[1792,128]{1,0:T(8,128)(2,1)S(1)} %bitcast.14, f32[192,512]{1,0:T(8,128)S(1)} %bitcast.19, ...), custom_call_target="tpu_custom_call" | custom-call | flops 1000000000 | bytes 1048576 | tf_op jit(solution)/shard_map/pallas_call | solution.py:340
  47.9 0.0 collective-permute-done
  48.0 0.0 collective-permute-done.1
  48.0 0.9 %shard_map.57 = bf16[128,8,128]{2,1,0:T(8,128)(2,1)S(1)} custom-call(bf16[192,128]{1,0:T(8,128)(2,1)S(1)} %bitcast.18, bf16[384,128]{1,0:T(8,128)(2,1)S(1)} %bitcast.17, bf16[512,192]{1,0:T(8,128)(2,1)S(1)} %get-tuple-element.19.vh_ref, bf16[512,192]{1,0:T(8,128)(2,1)S(1)} %get-tuple-element.20.vl_ref, bf16[192,512]{1,0:T(8,128)(2,1)S(1)} %get-tuple-element.21.ph_ref, ...), custom_call_target="tpu_custom_call" | custom-call | flops 1000000000 | bytes 1048576 | tf_op jit(solution)/shard_map/pallas_call | solution.py:354
  48.9 0.0 copy-start
  48.9 21.1 %all_to_all.11 = bf16[128,8,128]{2,1,0:T(8,128)(2,1)S(1)} all-to-all(bf16[128,8,128]{2,1,0:T(8,128)(2,1)S(1)} %shard_map.57), channel_id=1, replica_groups=mesh['x'=4,'y'=4,'mode'=32] {'y','mode'}, dimensions={0} | all-to-all | bytes 524288 | tf_op jit(solution)/shard_map/all_to_all | solution.py:312
  70.1 0.0 copy-done
  70.1 1.7 %shard_map.58 = bf16[6,128,128]{2,1,0:T(8,128)(2,1)} custom-call(bf16[4,32,8,128]{3,2,1,0:T(8,128)(2,1)S(1)} %bitcast.13, bf16[6,128,128]{2,1,0:T(8,128)(2,1)S(1)} %bitcast.16, bf16[512,512]{1,0:T(8,128)(2,1)S(1)} %get-tuple-element.25.swap, bf16[128,768]{1,0:T(8,128)(2,1)S(1)} %get-tuple-element.26.shift), custom_call_target="tpu_custom_call" | custom-call | flops 1000000 | bytes 1048576 | tf_op jit(solution)/shard_map/pallas_call | solution.py:361
  (1 shorter events, 0.0 us)
Async XLA Ops:
  1.7 43.7 %copy-start.1 = (f32[512,192]{0,1:T(8,128)S(1)}, f32[512,192]{0,1:T(8,128)}, u32[]{:S(2)}) copy-start(f32[512,192]{0,1:T(8,128)} %param.8) | copy-start | bytes 1179652
  38.9 9.1 %collective-permute-start.1 = (bf16[32,6,2,128]{3,2,1,0:T(2,128)(2,1)S(1)}, bf16[32,6,2,128]{3,2,1,0:T(2,128)(2,1)S(1)}, u32[]{:S(2)}, u32[]{:S(2)}) collective-permute-start(bf16[32,6,2,128]{3,2,1,0:T(2,128)(2,1)S(1)} %slice.9), channel_id=1, source_target_pairs={{384,0},{0,128},{128,256},{256,384},{385,1},{1,129},{129,257},{257... | collective-permute-start | bytes 294920 | tf_op jit(solution)/shard_map/ppermute | solution.py:308
  42.0 5.9 %collective-permute-start = (bf16[32,3,2,128]{3,2,1,0:T(2,128)(2,1)S(1)}, bf16[32,3,2,128]{3,2,1,0:T(2,128)(2,1)S(1)}, u32[]{:S(2)}, u32[]{:S(2)}) collective-permute-start(bf16[32,3,2,128]{3,2,1,0:T(2,128)(2,1)S(1)} %slice.8), channel_id=1, source_target_pairs={{128,0},{256,128},{384,256},{0,384},{129,1},{257,129},{385,257},{1... | collective-permute-start | bytes 147464 | tf_op jit(solution)/shard_map/ppermute | solution.py:308
  48.9 21.1 %copy-start = (bf16[6,1,128,128]{3,2,1,0:T(8,128)(2,1)S(1)}, bf16[6,1,128,128]{3,2,1,0:T(8,128)(2,1)}, u32[]{:S(2)}) copy-start(bf16[6,1,128,128]{3,2,1,0:T(8,128)(2,1)} %param.7) | copy-start | bytes 589828

commit v6 on v4

--- a/solution.py
+++ b/solution.py
@@ -245,12 +245,16 @@
     logs = values[:, X : 2 * X] + dot(vl_ref[...], faces[:, X : 2 * X])
     bottom = jnp.exp(logs) * (field_ref[:, 0:X] - values[:, 2 * X : 3 * X])
     both = project(ph_ref, jnp.concatenate([bottom, top], axis=1))
-    block[...] = block_ref[...]
+    outer = (slice(0, OWNERS), slice(3 * OWNERS, 4 * OWNERS))
+    for rows in outer:
+        block[rows] = block_ref[rows]
+    out_ref[OWNERS : 3 * OWNERS] = block_ref[OWNERS : 3 * OWNERS].astype(BF16)
     for m in range(OWN):
         modes = slice(m * OWNERS, (m + 1) * OWNERS)
         block[0:OWNERS, m, :] -= both[modes, 0:X]
         block[3 * OWNERS : 4 * OWNERS, m, :] += both[modes, X : 2 * X]
-    out_ref[...] = block[...].astype(BF16)
+    for rows in outer:
+        out_ref[rows] = block[rows].astype(BF16)
 
 
 def finish_kernel(got_ref, source_ref, swap, shift, out_any, wide, ring, cells, ends, flat, planes, sems):

time: 71.9 us -> 71.9 us (level)
  no operation moved by 1% of the time
where the time goes in v6:
time: 71.9 us; the launch traced here: 71.7 us
  blocking collectives  58 us (81%)
  Pallas kernels  6.97 us (10%)
  starting transfers between devices  6.49 us (9%)
    all_to_all x2, blocking collectives, exchange(): lax.all_to_all(block, ('y', 'mode'), split_axis=0, concat_axis=0, tiled=T...  58 us
    ppermute x2, starting transfers between devices, neighbour(): return lax.ppermute(block, 'x', route)  6.49 us
    pallas_call x1, Pallas kernels, shards(): call(own_kernel, [((Q, CELLS), F32), ((Q, CELLS), F32), ((group, 8, X), F...  2.39 us
    pallas_call x1, Pallas kernels, shards(): call(pack_kernel, [((group * SENT, X), BF16), ((Q, M), BF16), ((Q, M), BF...  2 us
    pallas_call x1, Pallas kernels, shards(): call(finish_kernel, [(plane, BF16)], [((ACROSS, DOWN, 8, X), F32), ((DOWN...  1.65 us
  transfers between devices with their start and end apart: 2, of which 0 were waited for; matrix products, arithmetic and copies ran while one was open for 0% of the time, Pallas kernels for 3%

profile of v6, /device:TPU:1, one launch (start us, length us, event | category | flops | bytes accessed | tf_op | source)
XLA Modules:
  0.0 71.7 jit_solution(8454542473420671320)
XLA Ops:
  0.0 2.0 %shard_map.55 = (bf16[1792,128]{1,0:T(8,128)(2,1)S(1)}, bf16[512,192]{1,0:T(8,128)(2,1)S(1)}, bf16[512,192]{1,0:T(8,128)(2,1)S(1)}, bf16[192,512]{1,0:T(8,128)(2...) custom-call(bf16[6,128,128]{2,1,0:T(8,128)(2,1)} %bitcast.20, ...), custom_call_target="tpu_custom_call" | custom-call | flops 1000000 | bytes 1048576 | tf_op jit(solution)/shard_map/pallas_call | solution.py:326
  2.0 36.9 %all_to_all.10 = bf16[128,7,2,128]{3,2,1,0:T(2,128)(2,1)S(1)} all-to-all(bf16[128,7,2,128]{3,2,1,0:T(2,128)(2,1)S(1)} %bitcast.15), channel_id=1, replica_groups=mesh['x'=4,'y'=4,'mode'=32] {'y','mode'}, dimensions={0} | all-to-all | bytes 917504 | tf_op jit(solution)/shard_map/all_to_all | solution.py:319
  38.9 0.1 slice.9
  39.0 3.1 %collective-permute-start.1 = (bf16[32,6,2,128]{3,2,1,0:T(2,128)(2,1)S(1)}, bf16[32,6,2,128]{3,2,1,0:T(2,128)(2,1)S(1)}, u32[]{:S(2)}, u32[]{:S(2)}) collective-permute-start(bf16[32,6,2,128]{3,2,1,0:T(2,128)(2,1)S(1)} %slice.9), channel_id=1, source_target_pairs={{384,0},{0,128},{128,256},{256,384},{385,1},{1,129},{129,257},{257... | collective-permute-start | bytes 294920 | tf_op jit(solution)/shard_map/ppermute | solution.py:315
  42.2 3.4 %collective-permute-start = (bf16[32,3,2,128]{3,2,1,0:T(2,128)(2,1)S(1)}, bf16[32,3,2,128]{3,2,1,0:T(2,128)(2,1)S(1)}, u32[]{:S(2)}, u32[]{:S(2)}) collective-permute-start(bf16[32,3,2,128]{3,2,1,0:T(2,128)(2,1)S(1)} %slice.8), channel_id=1, source_target_pairs={{128,0},{256,128},{384,256},{0,384},{129,1},{257,129},{385,257},{1... | collective-permute-start | bytes 147464 | tf_op jit(solution)/shard_map/ppermute | solution.py:315
  45.5 2.4 %shard_map.56 = (f32[512,512]{1,0:T(8,128)S(1)}, f32[512,512]{1,0:T(8,128)S(1)}, f32[128,8,128]{2,1,0:T(8,128)S(1)}) custom-call(bf16[1792,128]{1,0:T(8,128)(2,1)S(1)} %bitcast.14, bf16[512,192]{1,0:T(8,128)(2,1)S(1)} %get-tuple-element.16.vh_ref, bf16[512,192]{1,0:T(8,128)(2,1)S(1)} %get-tuple-element.17.vl_ref, ...), custom_call_target="tpu_custom_call" | custom-call | flops 1000000000 | bytes 1048576 | tf_op jit(solution)/shard_map/pallas_call | solution.py:351
  47.9 0.0 collective-permute-done
  47.9 0.0 collective-permute-done.1
  47.9 0.9 %shard_map.57 = bf16[128,8,128]{2,1,0:T(8,128)(2,1)S(1)} custom-call(bf16[192,128]{1,0:T(8,128)(2,1)S(1)} %bitcast.18, bf16[384,128]{1,0:T(8,128)(2,1)S(1)} %bitcast.17, bf16[512,192]{1,0:T(8,128)(2,1)S(1)} %get-tuple-element.16.vh_ref, bf16[512,192]{1,0:T(8,128)(2,1)S(1)} %get-tuple-element.17.vl_ref, bf16[192,512]{1,0:T(8,128)(2,1)S(1)} %get-tuple-element.18.ph_ref, ...), custom_call_target="tpu_custom_call" | custom-call | flops 1000000000 | bytes 1048576 | tf_op jit(solution)/shard_map/pallas_call | solution.py:361
  48.9 0.0 copy-start
  48.9 21.1 %all_to_all.11 = bf16[128,8,128]{2,1,0:T(8,128)(2,1)S(1)} all-to-all(bf16[128,8,128]{2,1,0:T(8,128)(2,1)S(1)} %shard_map.57), channel_id=1, replica_groups=mesh['x'=4,'y'=4,'mode'=32] {'y','mode'}, dimensions={0} | all-to-all | bytes 524288 | tf_op jit(solution)/shard_map/all_to_all | solution.py:319
  70.0 0.0 copy-done
  70.0 1.7 %shard_map.58 = bf16[6,128,128]{2,1,0:T(8,128)(2,1)} custom-call(bf16[4,32,8,128]{3,2,1,0:T(8,128)(2,1)S(1)} %bitcast.13, bf16[6,128,128]{2,1,0:T(8,128)(2,1)S(1)} %bitcast.16, bf16[512,512]{1,0:T(8,128)(2,1)S(1)} %get-tuple-element.23.swap, bf16[128,768]{1,0:T(8,128)(2,1)S(1)} %get-tuple-element.24.shift), custom_call_target="tpu_custom_call" | custom-call | flops 1000000 | bytes 1048576 | tf_op jit(solution)/shard_map/pallas_call | solution.py:368
  (1 shorter events, 0.0 us)
Async XLA Ops:
  39.0 9.0 %collective-permute-start.1 = (bf16[32,6,2,128]{3,2,1,0:T(2,128)(2,1)S(1)}, bf16[32,6,2,128]{3,2,1,0:T(2,128)(2,1)S(1)}, u32[]{:S(2)}, u32[]{:S(2)}) collective-permute-start(bf16[32,6,2,128]{3,2,1,0:T(2,128)(2,1)S(1)} %slice.9), channel_id=1, source_target_pairs={{384,0},{0,128},{128,256},{256,384},{385,1},{1,129},{129,257},{257... | collective-permute-start | bytes 294920 | tf_op jit(solution)/shard_map/ppermute | solution.py:315
  42.2 5.8 %collective-permute-start = (bf16[32,3,2,128]{3,2,1,0:T(2,128)(2,1)S(1)}, bf16[32,3,2,128]{3,2,1,0:T(2,128)(2,1)S(1)}, u32[]{:S(2)}, u32[]{:S(2)}) collective-permute-start(bf16[32,3,2,128]{3,2,1,0:T(2,128)(2,1)S(1)} %slice.8), channel_id=1, source_target_pairs={{128,0},{256,128},{384,256},{0,384},{129,1},{257,129},{385,257},{1... | collective-permute-start | bytes 147464 | tf_op jit(solution)/shard_map/ppermute | solution.py:315
  48.9 21.1 %copy-start = (bf16[6,1,128,128]{3,2,1,0:T(8,128)(2,1)S(1)}, bf16[6,1,128,128]{3,2,1,0:T(8,128)(2,1)}, u32[]{:S(2)}) copy-start(bf16[6,1,128,128]{3,2,1,0:T(8,128)(2,1)} %param.7) | copy-start | bytes 589828
